TPU v7x, 512 devices: a whole 4x8x8 slice. The times are simulated.
512 devices in a mesh: freq: 8 (over z), src: 64 (over y, x, core).
Axes of the slice: x: 4, y: 8, z: 8, core: 2. Of those that a mesh axis runs over, the one named last changes fastest.
Arguments:
- downgoing: float32 [16, 2048, 16384], P('freq', None, 'src'), parts along dimension 0, may hold values from -0.234375 to 0.234375
- upgoing: float32 [16, 16384, 128], P('freq', 'src'), parts along dimension 0, may hold values from -6 to 6
Outputs:
- reflectivity: float32 [2048, 16, 128], P('src', 'freq'), parts along dimension 1
- residual: float32 [16, 16384, 128], P('freq', 'src'), parts along dimension 0
There are 8 independent parts, one for each index of `freq`. A program takes and returns all parts, laid end to end along the dimension named above; each array names one. Nothing has to cross between parts.
All inputs are finite; a program needn't handle non-finite values.
Results may differ from a plain program's by a relative error of at most 0.0003.
Values sent between devices are 32-bit elements; how exact they have to be, the bound alone decides.
No kernel may reach another device: no remote copies, remote signals or barrier semaphores. Data moves between devices by JAX's collectives and lax.ppermute only.
A program may use at most 64 MiB of HBM per device.

v0:
```python
import jax
import jax.numpy as jnp
from jax import lax
from jax.sharding import PartitionSpec as P

ITERS = 2


HI = lax.Precision.HIGHEST


def contract_first(a, b):
    return lax.dot_general(
        a, b, (((0,), (0,)), ((), ())), precision=HI, preferred_element_type=jnp.float32
    )


def gradient_rows(downgoing, residual):
    real = jnp.dot(
        downgoing[0], residual[0], precision=HI, preferred_element_type=jnp.float32
    ) + jnp.dot(downgoing[1], residual[1], precision=HI, preferred_element_type=jnp.float32)
    imag = jnp.dot(
        downgoing[0], residual[1], precision=HI, preferred_element_type=jnp.float32
    ) - jnp.dot(downgoing[1], residual[0], precision=HI, preferred_element_type=jnp.float32)
    return jnp.stack([real, imag], axis=1)


def forward_rows(downgoing, piece):
    real = contract_first(downgoing[0], piece[:, 0]) - contract_first(downgoing[1], piece[:, 1])
    imag = contract_first(downgoing[0], piece[:, 1]) + contract_first(downgoing[1], piece[:, 0])
    return jnp.stack([real, imag])


def on_device(downgoing, upgoing):
    all_rows = downgoing.shape[1]
    rows = all_rows // lax.axis_size("src")
    width = upgoing.shape[2]
    residual = upgoing
    filt = jnp.zeros((rows, 2, width), jnp.float32)
    direction = filt
    gamma = jnp.float32(1.0)
    for step in range(ITERS):
        gradient = lax.psum_scatter(
            gradient_rows(downgoing, residual), "src", scatter_dimension=0, tiled=True
        )
        gamma_new = lax.psum(jnp.sum(gradient * gradient), "src")
        direction = gradient if step == 0 else gradient + gamma_new / gamma * direction
        gamma = gamma_new
        image = forward_rows(downgoing, lax.all_gather(direction, "src", axis=0, tiled=True))
        alpha = gamma / lax.psum(jnp.sum(image * image), "src")
        filt = filt + alpha * direction
        residual = residual - alpha * image
    return (filt, residual)


def solution(mesh):
    placed = (P("freq", None, "src"), P("freq", "src", None))
    return jax.shard_map(
        on_device,
        mesh=mesh,
        in_specs=placed,
        out_specs=(P("src", "freq", None), P("freq", "src", None)),
        check_vma=False,
    )
```

profile of v0, /device:TPU:1, one launch (start us, length us, event | category | flops | bytes accessed | tf_op | source)
XLA Modules:
  0.0 915.7 jit_solution(11871690116232581238)
XLA Ops:
  7.2 0.0 copy-start.6
  7.2 0.0 reduce-scatter.3.cloned.1.call-start
  7.2 0.0 copy-start
  7.2 3.6 fusion.28
  10.8 0.0 copy-done.6
  10.8 3.4 fusion.30
  14.3 0.0 copy-done
  14.3 1.9 fusion.2
  16.2 1.9 fusion.3
  18.1 1.5 pad_maximum_fusion
  19.5 0.0 reduce-scatter.3.cloned.1.call-update
  19.6 0.0 all-gather.3.cloned.1.call-start
  19.6 149.2 %reduce-scatter.3.cloned.1.call-done = f32[32,2,128]{2,0,1:T(8,128)} async-done(((f32[2048,2,128]{2,0,1:T(8,128)}), f32[32,2,128]{2,0,1:T(8,128)}) %reduce-scatter.3.cloned.1.call-update) | async-done | bytes 32784 | tf_op jit(solution)/shard_map/reduce_scatter | solution.py:43
  168.8 0.0 all-gather.3.cloned.1.call-update
  168.8 0.2 reduce-scatter.5.cloned.1.call-start
  169.1 1.4 multiply_reduce_fusion.3
  170.4 89.0 %all-gather.3.cloned.1.call-done = f32[2048,2,128]{2,0,1:T(8,128)} async-done(((f32[32,2,128]{2,0,1:T(8,128)}), f32[2048,2,128]{2,0,1:T(8,128)}) %all-gather.3.cloned.1.call-update) | async-done | bytes 2097168 | tf_op jit(solution)/shard_map/all_gather | solution.py:49
  259.4 0.0 copy-start.1
  259.4 3.9 fusion.10
  263.3 0.0 copy-start.4
  263.3 3.9 fusion.12
  267.2 0.0 copy-done.1
  267.3 0.0 copy-done.4
  267.3 2.0 fusion.57
  269.3 2.0 fusion.51
  271.2 0.7 multiply_reduce_fusion.1
  271.9 0.1 copy.4
  272.0 124.5 %all-reduce = (f32[]{:T(128)}, f32[]{:T(128)}) all-reduce(f32[]{:T(128)} %multiply_reduce_fusion.3, f32[]{:T(128)} %multiply_reduce_fusion.1), channel_id=1, replica_groups=mesh['freq'=8,'src'=64] {'src'}, use_global_device_ids=true, to_apply=%region_2.0 | all-reduce | flops 2 | bytes 16 | tf_op jit(solution)/shard_map/psum | solution.py:46
  397.9 0.0 copy-start.2
  397.9 3.6 fusion.20
  401.5 3.4 fusion.22
  405.0 0.0 copy-done.2
  405.0 1.9 fusion
  406.9 1.9 fusion.1
  408.9 1.5 pad_maximum_fusion.1
  410.4 0.0 copy-start.7
  410.4 0.0 reduce-scatter.5.cloned.1.call-update
  410.4 0.0 all-gather.5.cloned.1.call-start
  410.4 144.0 %reduce-scatter.5.cloned.1.call-done = f32[32,2,128]{2,0,1:T(8,128)} async-done(((f32[2048,2,128]{2,0,1:T(8,128)}), f32[32,2,128]{2,0,1:T(8,128)}) %reduce-scatter.5.cloned.1.call-update) | async-done | bytes 32784 | tf_op jit(solution)/shard_map/reduce_scatter | solution.py:43
  554.4 1.4 multiply_reduce_fusion.2
  555.8 130.1 %psum.30 = f32[]{:T(128)} all-reduce(f32[]{:T(128)} %multiply_reduce_fusion.2), channel_id=1, replica_groups=mesh['freq'=8,'src'=64] {'src'}, use_global_device_ids=true, to_apply=%region_7.0 | all-reduce | flops 1 | bytes 8 | tf_op jit(solution)/shard_map/psum | solution.py:46
  687.2 0.0 copy-done.7
  687.2 1.4 multiply_add_fusion.1
  688.6 0.0 all-gather.5.cloned.1.call-update
  688.6 80.9 %all-gather.5.cloned.1.call-done = f32[2048,2,128]{2,0,1:T(8,128)} async-done(((f32[32,2,128]{2,0,1:T(8,128)}), f32[2048,2,128]{2,0,1:T(8,128)}) %all-gather.5.cloned.1.call-update) | async-done | bytes 2097168 | tf_op jit(solution)/shard_map/all_gather | solution.py:49
  769.5 0.0 copy-start.3
  769.5 3.9 fusion.4
  773.4 0.0 copy-start.5
  773.4 3.9 fusion.6
  777.3 0.0 copy-done.3
  777.3 0.0 copy-done.5
  777.3 2.0 fusion.69
  779.3 0.0 copy-start.8
  779.3 2.0 fusion.63
  781.3 0.7 multiply_reduce_fusion
  782.1 124.2 %psum.31 = f32[]{:T(128)} all-reduce(f32[]{:T(128)} %multiply_reduce_fusion), channel_id=1, replica_groups=mesh['freq'=8,'src'=64] {'src'}, use_global_device_ids=true, to_apply=%region_9.0 | all-reduce | flops 1 | bytes 8 | tf_op jit(solution)/shard_map/psum | solution.py:50
  907.6 0.1 multiply_subtract_fusion
  907.7 0.0 copy-done.8
  907.7 0.6 copy.9
  908.4 0.8 copy.10
  (2 shorter events, 0.0 us)
Async XLA Ops:
  7.2 3.7 copy-start.6
  7.2 161.6 %reduce-scatter.3.cloned.1.call-start = ((), (), s32[]{:S(2)}) async-start(), calls=%async_computation.2 | async-start | bytes 2129920 | tf_op jit(solution)/shard_map/reduce_scatter | solution.py:43
  7.2 7.1 copy-start
  19.6 239.8 %all-gather.3.cloned.1.call-start = ((), (), s32[]{:S(2)}) async-start(), calls=%async_computation.3 | async-start | bytes 2129920 | tf_op jit(solution)/shard_map/all_gather | solution.py:49
  168.8 385.6 %reduce-scatter.5.cloned.1.call-start = ((), (), s32[]{:S(2)}) async-start(), calls=%async_computation.4 | async-start | bytes 2129920 | tf_op jit(solution)/shard_map/reduce_scatter | solution.py:43
  259.4 7.8 copy-start.1
  263.3 3.9 copy-start.4
  397.9 7.0 copy-start.2
  410.4 276.8 %copy-start.7 = (f32[32,2,128]{2,0,1:T(8,128)S(1)}, f32[32,2,128]{2,0,1:T(8,128)}, u32[]{:S(2)}) copy-start(f32[32,2,128]{2,0,1:T(8,128)} %reduce-scatter.3.cloned.1.call-done) | copy-start | bytes 98308
  410.4 359.1 %all-gather.5.cloned.1.call-start = ((), (), s32[]{:S(2)}) async-start(), calls=%async_computation.5 | async-start | bytes 2129920 | tf_op jit(solution)/shard_map/all_gather | solution.py:49
  769.5 7.8 copy-start.3
  773.4 3.9 copy-start.5
  779.3 128.4 %copy-start.8 = (f32[32,2,128]{2,0,1:T(8,128)S(1)}, f32[32,2,128]{2,0,1:T(8,128)}, u32[]{:S(2)}) copy-start(f32[32,2,128]{2,0,1:T(8,128)} %multiply_add_fusion.1) | copy-start | bytes 98308
Sparse Core Ops, SparseCore 0:
  19.7 149.0 reduce-scatter.2
  172.7 86.6 all-gather.2
  410.5 143.8 reduce-scatter.4
  688.7 80.7 all-gather.4
where the time goes:
time: 917 us; the launch traced here: 916 us
  waiting for transfers between devices  463 us (50%)
  blocking collectives  379 us (41%)
  matrix products  45.2 us (5%)
  between operations  18.1 us (2%)
    reduce_scatter x2, waiting for transfers between devices, on_device(): lax.psum_scatter(gradient_rows(downgoing, residual), 'src', scatter_dimen...  293 us
    psum x2, blocking collectives, on_device(): gamma_new = lax.psum(jnp.sum(gradient * gradient), 'src')  255 us
    all_gather x2, waiting for transfers between devices, on_device(): lax.all_gather(direction, 'src', axis=0, tiled=True)  170 us
    psum x1, blocking collectives, on_device(): alpha = gamma / lax.psum(jnp.sum(image * image), 'src')  124 us
    dot_general x8, matrix products, contract_first(): lax.dot_general(a, b, (((0,), (0,)), ((), ())), precision=HI, preferred_e...  23.5 us
  transfers between devices with their start and end apart: 4, of which 4 were waited for; matrix products, arithmetic and copies ran while one was open for 0% of the time, Pallas kernels for 0%

commit v1 on v0

v1 whole, which is shorter than its diff:
```python
import jax
import jax.numpy as jnp
from jax import lax
from jax.sharding import PartitionSpec as P

HI = lax.Precision.HIGH
CHIPS = 32
SAME_CORE = [[2 * j + c for j in range(CHIPS)] for c in range(2)]
SWAP = [(i, i ^ 1) for i in range(2 * CHIPS)]


def dot(a, b, dims):
    return lax.dot_general(a, b, ((dims[0], dims[1]), ((), ())), precision=HI, preferred_element_type=jnp.float32)


def exchange(blocks):
    return lax.all_to_all(blocks, "src", 0, 0, axis_index_groups=SAME_CORE, tiled=True)


def pack(re, im):
    return jnp.concatenate([re[:, :64], im[:, :64]], 1), jnp.concatenate([re[:, 64:], im[:, 64:]], 1)


def turn(z):
    return jnp.concatenate([-z[:, 64:], z[:, :64]], 1)


def adjoint(down, field):
    return dot(down[0], field, ((1,), (0,))) - dot(down[1], turn(field), ((1,), (0,)))


def forward(down, piece):
    return dot(down[0], piece, ((0,), (0,))) + dot(down[1], turn(piece), ((0,), (0,)))


def all_sum(partial):
    rows = partial.shape[0]
    parts = exchange(partial.reshape(CHIPS, rows // CHIPS, 128))
    block = jnp.sum(parts, axis=0)
    return exchange(jnp.broadcast_to(block, parts.shape)).reshape(rows, 128)


def ratio(a, b, other):
    good = b > 0
    return jnp.where(good, a / jnp.where(good, b, 1.0), other)


def on_device(downgoing, upgoing):
    core = lax.axis_index("src") % 2
    chip = lax.axis_index("src") // 2
    lower = core == 0
    low, high = pack(upgoing[0], upgoing[1])
    mine, theirs = jnp.where(lower, low, high), jnp.where(lower, high, low)
    both = adjoint(downgoing, mine), adjoint(downgoing, theirs)
    partial = both[0] + lax.ppermute(both[1], "src", SWAP)
    other_down = lax.ppermute(downgoing, "src", SWAP)
    g0 = all_sum(partial)

    image0_own, image0_other = forward(downgoing, g0), forward(other_down, g0)
    q = all_sum(adjoint(downgoing, image0_own) + adjoint(other_down, image0_other))

    gamma0 = jnp.sum(g0 * g0)
    m1 = jnp.sum(g0 * q)
    a = ratio(gamma0, m1, 1.0)
    g1 = g0 - a * q
    gamma1 = jnp.sum(g1 * g1)
    beta = ratio(gamma1, gamma0, 0.0)
    p1 = g1 + beta * g0
    image1_own, image1_other = forward(downgoing, p1), forward(other_down, p1)
    square = jnp.sum(image1_own * image1_own) + jnp.sum(image1_other * image1_other)

    lane = lax.broadcasted_iota(jnp.int32, (2 * CHIPS, 8, 128), 2)
    row = jnp.where(lane == 0, square, jnp.where(lane == 1, gamma0, jnp.where(lane == 2, m1, gamma1)))
    got = lax.all_to_all(row, "src", 0, 0, tiled=True)[:, 0]
    sq = jnp.sum(got[:, 0].reshape(CHIPS, 2), axis=0)
    ga0, m, ga1 = got[:2, 1], got[:2, 2], got[:2, 3]

    ac = ratio(ga0, m, 1.0)
    bc = ratio(ga1, ga0, 0.0)
    gamma = jnp.sum(ga0)
    alpha0 = gamma / jnp.sum(m)
    s = alpha0 / ac
    gamma_new = jnp.sum(s * s * ga1 + (1.0 - s) * (1.0 - s) * ga0)
    e = gamma_new / gamma + 1.0 - s - s * bc
    alpha1 = gamma_new / jnp.sum(s * s * sq + e * e * m)
    k0 = alpha0 + alpha1 * e
    k1 = alpha1 * s

    def halves(k):
        return jnp.where(lower, k[0], k[1]), jnp.where(lower, k[1], k[0])

    mine0, theirs0 = halves(k0)
    mine1, theirs1 = halves(k1)

    def rows32(z, which):
        return lax.dynamic_slice_in_dim(z, chip * 64 + 32 * which, 32, 0)

    give = jnp.concatenate([image0_other, image1_other, rows32(g0, 1 - core), rows32(p1, 1 - core)], 0)
    take = lax.ppermute(give, "src", SWAP)
    image0_take, image1_take, g0_take, p1_take = take[:256], take[256:512], take[512:544], take[544:]

    def out(mine, theirs):
        low, high = jnp.where(lower, mine, theirs), jnp.where(lower, theirs, mine)
        return jnp.concatenate([low[:, :64], high[:, :64]], 1), jnp.concatenate([low[:, 64:], high[:, 64:]], 1)

    res_mine = mine - mine0 * image0_own - mine1 * image1_own
    res_theirs = theirs - theirs0 * image0_take - theirs1 * image1_take
    residual = jnp.stack(out(res_mine, res_theirs))
    filt = jnp.stack(
        out(mine0 * rows32(g0, core) + mine1 * rows32(p1, core), theirs0 * g0_take + theirs1 * p1_take), axis=1
    )
    return (filt, residual)


def solution(mesh):
    placed = (P("freq", None, "src"), P("freq", "src", None))
    return jax.shard_map(
        on_device,
        mesh=mesh,
        in_specs=placed,
        out_specs=(P("src", "freq", None), P("freq", "src", None)),
        check_vma=False,
    )
```

time: 917 us -> 229 us (0.25)
  waiting for transfers between devices: 463 us -> 58.5 us
  blocking collectives: 379 us -> 63.4 us
  starting transfers between devices: 0.34 us -> 35.9 us
  matrix products: 45.2 us -> 30.8 us
  local copies, waits for them, and re-layouts: 1.65 us -> 12.2 us
    psum x3 -> x0, blocking collectives: 379 us -> none  [the longest x2 255 us: on_device(): gamma_new = lax.psum(jnp.sum(gradient * gradient), 'src')]
    reduce_scatter x2 -> x0, waiting for transfers between devices: 293 us -> none  [on_device(): lax.psum_scatter(gradient_rows(downgoing, residual), 'src', scatter_dimen...]
    all_gather x2 -> x0, waiting for transfers between devices: 170 us -> none  [on_device(): lax.all_gather(direction, 'src', axis=0, tiled=True)]
    all_to_all x0 -> x2, blocking collectives: none -> 63.4 us  [exchange(): lax.all_to_all(blocks, 'src', 0, 0, axis_index_groups=SAME_CORE, tiled=True)]
    all_to_all x0 -> x3, waiting for transfers between devices: none -> 57.4 us  [the longest x2 47.8 us: exchange(): lax.all_to_all(blocks, 'src', 0, 0, axis_index_groups=SAME_CORE, tiled=True)]
    all_to_all x0 -> x3, starting transfers between devices: none -> 22.1 us  [the longest x2 11.9 us: exchange(): lax.all_to_all(blocks, 'src', 0, 0, axis_index_groups=SAME_CORE, tiled=True)]
    dot_general x16, matrix products: 45.2 us -> 30.8 us  [dot(): lax.dot_general(a, b, ((dims[0], dims[1]), ((), ())), precision=HI, prefe...]
    ppermute x0 -> x3, starting transfers between devices: none -> 13.8 us  [the longest x1 8.79 us: on_device(): partial = both[0] + lax.ppermute(both[1], 'src', SWAP)]
  transfers between devices with their start and end apart: 4 -> 6, of which waited for: 4 -> 4; matrix products, arithmetic and copies ran while one was open for 0% -> 5% of each run, Pallas kernels for 0% -> 0%
where the time goes in v1:
time: 229 us; the launch traced here: 228 us
  blocking collectives  63.4 us (28%)
  waiting for transfers between devices  58.5 us (26%)
  starting transfers between devices  35.9 us (16%)
  matrix products  30.8 us (13%)
  between operations  15.5 us (7%)
  local copies, waits for them, and re-layouts  12.2 us (5%)
  other arithmetic  11.3 us (5%)
    all_to_all x2, blocking collectives, exchange(): lax.all_to_all(blocks, 'src', 0, 0, axis_index_groups=SAME_CORE, tiled=True)  63.4 us
    all_to_all x2, waiting for transfers between devices, exchange(): lax.all_to_all(blocks, 'src', 0, 0, axis_index_groups=SAME_CORE, tiled=True)  47.8 us
    dot_general x16, matrix products, dot(): lax.dot_general(a, b, ((dims[0], dims[1]), ((), ())), precision=HI, prefe...  30.8 us
    all_to_all x2, starting transfers between devices, exchange(): lax.all_to_all(blocks, 'src', 0, 0, axis_index_groups=SAME_CORE, tiled=True)  11.9 us
    all_to_all x1, starting transfers between devices, on_device(): got = lax.all_to_all(row, 'src', 0, 0, tiled=True)[:, 0]  10.3 us
    all_to_all x1, waiting for transfers between devices, on_device(): got = lax.all_to_all(row, 'src', 0, 0, tiled=True)[:, 0]  9.62 us
    ppermute x1, starting transfers between devices, on_device(): partial = both[0] + lax.ppermute(both[1], 'src', SWAP)  8.79 us
  transfers between devices with their start and end apart: 6, of which 4 were waited for; matrix products, arithmetic and copies ran while one was open for 5% of the time, Pallas kernels for 0%

profile of v1, /device:TPU:1, one launch (start us, length us, event | category | flops | bytes accessed | tf_op | source)
XLA Modules:
  0.0 227.5 jit_solution(3748915790514707619)
XLA Ops:
  0.6 1.0 fusion.77
  1.6 0.1 copy.49
  1.7 0.1 copy.50
  1.9 2.9 %fusion.18 = f32[128,2048]{1,0:T(8,128)S(1)} fusion(f32[256,128]{0,1:T(8,128)S(1)} %get-tuple-element.34, f32[2,2048,256]{2,1,0:T(8,128)} %param.2), kind=kOutput, calls=%fused_computation.24 | convolution fusion | flops 402653184 | bytes 3276800 | tf_op jit(solution)/shard_map/dot_general | solution.py:13
  4.9 1.2 fusion.2
  6.1 8.8 %collective-permute-start = (f32[2048,128]{0,1:T(8,128)S(1)}, f32[2048,128]{0,1:T(8,128)S(1)}, u32[]{:S(2)}, u32[]{:S(2)}) collective-permute-start(f32[2048,128]{0,1:T(8,128)S(1)} %fusion.2), channel_id=1, source_target_pairs={{0,1},{1,0},{2,3},{3,2},{4,5},{5,4},{6,7},{7,6},{8,9},{9,8},{10,11... | collective-permute-start | bytes 3145736 | tf_op jit(solution)/shard_map/ppermute | solution.py:55
  14.9 1.2 fusion.20
  16.1 1.0 collective-permute-done
  17.1 1.2 fusion.4
  18.4 1.3 copy.36
  19.7 4.3 %all-to-all-start = ((f32[32,64,128]{2,1,0:T(8,128)}), f32[32,64,128]{2,1,0:T(8,128)S(1)}, u32[]{:S(2)}, u32[]{:S(2)}) async-start(f32[32,64,128]{2,1,0:T(8,128)} %bitcast.6), calls=%async_computation | async-start | bytes 2097152 | tf_op jit(solution)/shard_map/all_to_all | solution.py:17
  24.0 2.6 %collective-permute-start.1 = (f32[2,2048,256]{2,1,0:T(8,128)}, f32[2,2048,256]{2,1,0:T(8,128)}, u32[]{:S(2)}, u32[]{:S(2)}) collective-permute-start(f32[2,2048,256]{2,1,0:T(8,128)} %param.2), channel_id=1, source_target_pairs={{0,1},{1,0},{2,3},{3,2},{4,5},{5,4},{6,7},{7,6},{8,9},{9,8},{10,11... | collective-permute-start | bytes 12582920 | tf_op jit(solution)/shard_map/ppermute | solution.py:56
  26.6 23.8 %all-to-all-done = f32[32,64,128]{2,1,0:T(8,128)S(1)} async-done(((f32[32,64,128]{2,1,0:T(8,128)}), f32[32,64,128]{2,1,0:T(8,128)S(1)}, u32[]{:S(2)}, u32[]{:S(2)}) %all-to-all-start) | async-done | bytes 1048608 | tf_op jit(solution)/shard_map/all_to_all | solution.py:17
  50.3 0.1 reduce_sum.108
  50.4 0.1 broadcast_in_dim.28
  50.5 32.2 %all_to_all.25 = f32[32,64,128]{2,1,0:T(8,128)S(1)} all-to-all(f32[32,64,128]{2,1,0:T(8,128)S(1)} %broadcast_in_dim.28), channel_id=1, replica_groups={{0,2,4,6,8,10,12,14,16,18,20,22,24,26,28,30,32,34,36,38,40,42,44,46,48,..., dimensions={0} | all-to-all | bytes 2097152 | tf_op jit(solution)/shard_map/all_to_all | solution.py:17
  82.8 0.3 slice_negate_fusion
  83.1 1.5 fusion.8
  84.6 1.1 fusion.40
  85.7 1.2 fusion.14
  87.0 3.0 %fusion.26 = f32[128,256]{1,0:T(8,128)S(1)} fusion(f32[2,2048,256]{2,1,0:T(8,128)} %collective-permute-done.1, f32[2048,64]{1,0:T(8,128)S(1)} %get-tuple-element.32, f32[2048,64]{1,0:T(8,128)S(1)} %get-tuple-element.31), kind=kOutput, calls=%fused_computation.32 | convolution fusion | flops 402915328 | bytes 3276800 | tf_op jit(solution)/shard_map/dot_general | solution.py:13
  89.9 2.6 %fusion.37 = f32[128,256]{1,0:T(8,128)S(1)} fusion(f32[128,256]{1,0:T(8,128)S(1)} %fusion.26, f32[2048,128]{1,0:T(8,128)S(1)} %bitcast.93, f32[2,2048,256]{2,1,0:T(8,128)} %collective-permute-done.1), kind=kOutput, calls=%fused_computation.43 | convolution fusion | flops 402685952 | bytes 3407872 | tf_op jit(solution)/shard_map/dot_general | solution.py:13
  92.6 1.2 convolution_subtract_fusion.1
  93.8 2.8 %fusion.25 = f32[128,2048]{1,0:T(8,128)S(1)} fusion(f32[2,2048,256]{2,1,0:T(8,128)} %collective-permute-done.1, f32[256,64]{0,1:T(8,128)S(1)} %get-tuple-element.42, f32[256,64]{0,1:T(8,128)S(1)} %get-tuple-element.41), kind=kOutput, calls=%fused_computation.31 | convolution fusion | flops 402685952 | bytes 3276800 | tf_op jit(solution)/shard_map/dot_general | solution.py:13
  96.6 2.8 %fusion.1 = f32[2048,128]{0,1:T(8,128)S(1)} fusion(f32[128,2048]{1,0:T(8,128)S(1)} %convolution_subtract_fusion.1, f32[128,2048]{1,0:T(8,128)S(1)} %fusion.25, f32[128,256]{1,0:T(8,128)S(1)} %fusion.37, f32[2,2048,256]{2,1,0:T(8,128)} %collective-permute-done.1), kind=kOutput, calls=%fused_computation.2 | convolution fusion | flops 403177472 | bytes 5373952 | tf_op jit(solution)/shard_map/dot_general | solution.py:13
  99.4 0.3 copy.37
  99.7 31.1 %all_to_all.26 = f32[32,64,128]{2,1,0:T(8,128)S(1)} all-to-all(f32[32,64,128]{2,1,0:T(8,128)S(1)} %bitcast.98), channel_id=1, replica_groups={{0,2,4,6,8,10,12,14,16,18,20,22,24,26,28,30,32,34,36,38,40,42,44,46,48,..., dimensions={0} | all-to-all | bytes 2097152 | tf_op jit(solution)/shard_map/all_to_all | solution.py:17
  130.8 0.1 reduce_sum.109
  130.9 1.1 broadcast_in_dim.29
  132.0 7.6 %all-to-all-start.3 = ((f32[32,64,128]{2,1,0:T(8,128)}), f32[32,64,128]{2,1,0:T(8,128)S(1)}, u32[]{:S(2)}, u32[]{:S(2)}) async-start(f32[32,64,128]{2,1,0:T(8,128)} %broadcast_in_dim.29), calls=%async_computation.3 | async-start | bytes 2097152 | tf_op jit(solution)/shard_map/all_to_all | solution.py:17
  139.6 0.3 copy.38
  139.9 24.1 %all-to-all-done.3 = f32[32,64,128]{2,1,0:T(8,128)S(1)} async-done(((f32[32,64,128]{2,1,0:T(8,128)}), f32[32,64,128]{2,1,0:T(8,128)S(1)}, u32[]{:S(2)}, u32[]{:S(2)}) %all-to-all-start.3) | async-done | bytes 1048608 | tf_op jit(solution)/shard_map/all_to_all | solution.py:17
  164.0 0.9 multiply_reduce_fusion.1
  168.2 2.2 multiply_reduce_fusion
  170.4 1.2 compare_select_fusion.4
  172.2 2.6 %copy.39 = f32[2048,128]{0,1:T(8,128)} copy(f32[2048,128]{1,0:T(8,128)} %bitcast.97) | data formatting | bytes 2097152 | tf_op jit(solution)/shard_map/mul | solution.py:65
  174.8 1.5 multiply_add_fusion
  176.3 0.1 slice_negate_fusion.1
  176.4 0.9 copy-done.2
  177.3 0.8 fusion.5
  178.1 0.2 multiply_add_fusion.1
  178.3 1.7 multiply_reduce_fusion.4
  180.0 2.3 %fusion.24 = f32[128,256]{1,0:T(8,128)S(1)} fusion(f32[2,2048,256]{2,1,0:T(8,128)} %collective-permute-done.1, f32[2048,64]{0,1:T(8,128)S(1)} %get-tuple-element.30, f32[2048,64]{0,1:T(8,128)S(1)} %get-tuple-element.29), kind=kOutput, calls=%fused_computation.30 | convolution fusion | flops 402915328 | bytes 3276800 | tf_op jit(solution)/shard_map/dot_general | solution.py:13
  182.4 3.3 %multiply_reduce_fusion.3 = (f32[]{:T(128)}, f32[256,128]{0,1:T(8,128)S(1)}) fusion(f32[128,256]{1,0:T(8,128)S(1)} %fusion.24, f32[2048,128]{1,0:T(8,128)S(1)} %bitcast.96, f32[2,2048,256]{2,1,0:T(8,128)} %collective-permute-done.1), kind=kOutput, calls=%fused_computation.82 | convolution fusion | flops 402751488 | bytes 3407876 | tf_op jit(solution)/shard_map/dot_general | solution.py:13
  186.9 1.4 select_select_fusion
  188.3 10.3 %all-to-all-start.4 = ((f32[64,8,128]{2,1,0:T(8,128)}), f32[64,8,128]{2,1,0:T(8,128)}, u32[]{:S(2)}, u32[]{:S(2)}) async-start(f32[64,8,128]{2,1,0:T(8,128)} %select_select_fusion), calls=%async_computation.4 | async-start | bytes 524288 | tf_op jit(solution)/shard_map/all_to_all | solution.py:74
  198.6 0.1 constant_dynamic-slice_fusion
  198.7 0.1 constant_dynamic-slice_fusion.1
  198.8 0.8 pad_maximum_fusion.6
  199.6 2.4 %collective-permute-start.2 = (f32[576,128]{0,1:T(8,128)}, f32[576,128]{0,1:T(8,128)S(1)}, u32[]{:S(2)}, u32[]{:S(2)}) collective-permute-start(f32[576,128]{0,1:T(8,128)} %pad_maximum_fusion.6), channel_id=1, source_target_pairs={{0,1},{1,0},{2,3},{3,2},{4,5},{5,4},{6,7},{7,6},{8,9},{9,8},{10,11... | collective-permute-start | bytes 884744 | tf_op jit(solution)/shard_map/ppermute | solution.py:99
  202.0 9.6 %all-to-all-done.4 = f32[64,8,128]{2,1,0:T(8,128)} async-done(((f32[64,8,128]{2,1,0:T(8,128)}), f32[64,8,128]{2,1,0:T(8,128)}, u32[]{:S(2)}, u32[]{:S(2)}) %all-to-all-start.4) | async-done | bytes 262176 | tf_op jit(solution)/shard_map/all_to_all | solution.py:74
  211.6 1.0 slice.210
  212.6 0.1 slice_reduce_fusion
  212.7 0.8 slice_reduce_fusion.1
  214.8 0.6 add_reduce_fusion.1
  216.8 0.1 reshape_squeeze.3
  216.9 0.6 add_reduce_fusion
  218.9 0.6 fusion.85
  222.1 0.6 fusion.84
  225.3 0.1 broadcast_select_fusion.3
  225.8 0.1 maximum_bitcast_fusion.2
  225.9 0.1 maximum_bitcast_fusion.3
  225.9 0.6 copy.47
  226.7 0.8 copy.48
  (37 shorter events, 0.6 us)
Async XLA Ops:
  1.8 3.0 %copy-start = (f32[2,2048,256]{2,1,0:T(8,128)S(1)}, f32[2,2048,256]{2,1,0:T(8,128)}, u32[]{:S(2)}) copy-start(f32[2,2048,256]{2,1,0:T(8,128)} %param.2) | copy-start | bytes 12582916
  6.1 11.1 %collective-permute-start = (f32[2048,128]{0,1:T(8,128)S(1)}, f32[2048,128]{0,1:T(8,128)S(1)}, u32[]{:S(2)}, u32[]{:S(2)}) collective-permute-start(f32[2048,128]{0,1:T(8,128)S(1)} %fusion.2), channel_id=1, source_target_pairs={{0,1},{1,0},{2,3},{3,2},{4,5},{5,4},{6,7},{7,6},{8,9},{9,8},{10,11... | collective-permute-start | bytes 3145736 | tf_op jit(solution)/shard_map/ppermute | solution.py:55
  19.7 30.6 %all-to-all-start = ((f32[32,64,128]{2,1,0:T(8,128)}), f32[32,64,128]{2,1,0:T(8,128)S(1)}, u32[]{:S(2)}, u32[]{:S(2)}) async-start(f32[32,64,128]{2,1,0:T(8,128)} %bitcast.6), calls=%async_computation | async-start | bytes 2097152 | tf_op jit(solution)/shard_map/all_to_all | solution.py:17
  24.0 62.9 %collective-permute-start.1 = (f32[2,2048,256]{2,1,0:T(8,128)}, f32[2,2048,256]{2,1,0:T(8,128)}, u32[]{:S(2)}, u32[]{:S(2)}) collective-permute-start(f32[2,2048,256]{2,1,0:T(8,128)} %param.2), channel_id=1, source_target_pairs={{0,1},{1,0},{2,3},{3,2},{4,5},{5,4},{6,7},{7,6},{8,9},{9,8},{10,11... | collective-permute-start | bytes 12582920 | tf_op jit(solution)/shard_map/ppermute | solution.py:56
  50.4 32.7 %copy-start.1 = (f32[2,2048,256]{2,1,0:T(8,128)S(1)}, f32[2,2048,256]{2,1,0:T(8,128)}, u32[]{:S(2)}) copy-start(f32[2,2048,256]{2,1,0:T(8,128)} %param.2) | copy-start | bytes 12582916
  92.5 4.0 %copy-start.4 = (f32[128,256]{1,0:T(8,128)}, f32[128,256]{1,0:T(8,128)S(1)}, u32[]{:S(2)}) copy-start(f32[128,256]{1,0:T(8,128)S(1)} %fusion.37) | copy-start | bytes 393220
  132.0 32.0 %all-to-all-start.3 = ((f32[32,64,128]{2,1,0:T(8,128)}), f32[32,64,128]{2,1,0:T(8,128)S(1)}, u32[]{:S(2)}, u32[]{:S(2)}) async-start(f32[32,64,128]{2,1,0:T(8,128)} %broadcast_in_dim.29), calls=%async_computation.3 | async-start | bytes 2097152 | tf_op jit(solution)/shard_map/all_to_all | solution.py:17
  174.8 2.5 %copy-start.2 = (f32[2,2048,256]{2,1,0:T(8,128)S(1)}, f32[2,2048,256]{2,1,0:T(8,128)}, u32[]{:S(2)}) copy-start(f32[2,2048,256]{2,1,0:T(8,128)} %param.2) | copy-start | bytes 12582916
  174.8 3.3 %copy-start.3 = (f32[32,64,128]{2,1,0:T(8,128)S(1)}, f32[32,64,128]{2,1,0:T(8,128)}, u32[]{:S(2)}) copy-start(f32[32,64,128]{2,1,0:T(8,128)} %get-tuple-element.25) | copy-start | bytes 3145732
  180.0 18.8 %copy-start.5 = (f32[128,256]{1,0:T(8,128)S(1)}, f32[128,256]{1,0:T(8,128)}, u32[]{:S(2)}) copy-start(f32[128,256]{1,0:T(8,128)} %copy-done.4) | copy-start | bytes 393220
  188.3 23.4 %all-to-all-start.4 = ((f32[64,8,128]{2,1,0:T(8,128)}), f32[64,8,128]{2,1,0:T(8,128)}, u32[]{:S(2)}, u32[]{:S(2)}) async-start(f32[64,8,128]{2,1,0:T(8,128)} %select_select_fusion), calls=%async_computation.4 | async-start | bytes 524288 | tf_op jit(solution)/shard_map/all_to_all | solution.py:74
  199.6 25.7 %collective-permute-start.2 = (f32[576,128]{0,1:T(8,128)}, f32[576,128]{0,1:T(8,128)S(1)}, u32[]{:S(2)}, u32[]{:S(2)}) collective-permute-start(f32[576,128]{0,1:T(8,128)} %pad_maximum_fusion.6), channel_id=1, source_target_pairs={{0,1},{1,0},{2,3},{3,2},{4,5},{5,4},{6,7},{7,6},{8,9},{9,8},{10,11... | collective-permute-start | bytes 884744 | tf_op jit(solution)/shard_map/ppermute | solution.py:99

commit v2 on v0

v2 whole, which is shorter than its diff:
```python
import functools

import jax
import jax.numpy as jnp
from jax import lax
from jax.experimental import pallas as pl
from jax.experimental.pallas import tpu as pltpu
from jax.sharding import Mesh, PartitionSpec as P

SRC = ("y", "x", "core")
CHIPS = 32
ROWS = 2048
OWN = 256
STEP = 256
STEPS = ROWS // STEP
SWAP = [(i, i ^ 1) for i in range(2 * CHIPS)]
VMEM = pl.BlockSpec(memory_space=pltpu.VMEM)
SMEM = pl.BlockSpec(memory_space=pltpu.SMEM)
PARAMS = pltpu.CompilerParams(vmem_limit_bytes=56 * 2**20)
F32 = jnp.float32
BF16 = jnp.bfloat16


def dot(a, b):
    return jnp.dot(a, b, preferred_element_type=F32)


def split(x):
    high = x.astype(BF16)
    return high, (x - high.astype(F32)).astype(BF16)


def lanes(x):
    return lax.broadcasted_iota(jnp.int32, x.shape, x.ndim - 1) < 64


def turn(z):
    swapped = pltpu.roll(z, 64, 1)
    return jnp.where(lanes(z), -swapped, swapped)


def halves(re, im):
    first = lanes(re)
    return jnp.where(first, re, pltpu.roll(im, 64, 1)), jnp.where(first, pltpu.roll(re, 64, 1), im)


def ratio(a, b, other):
    good = b > 0
    return jnp.where(good, a / jnp.where(good, b, 1.0), other)


def first_kernel(core_ref, down_ref, up_ref, mine_ref, theirs_ref, high_ref, low_ref):
    @pl.when(pl.program_id(0) == 0)
    def _():
        lower, upper = halves(up_ref[0], up_ref[1])
        swap = core_ref[0] == 1
        for k, half in enumerate((jnp.where(swap, upper, lower), jnp.where(swap, lower, upper))):
            cols = slice(128 * k, 128 * k + 128)
            for rows, field in ((slice(0, OWN), half), (slice(OWN, 2 * OWN), -turn(half))):
                high, low = split(field)
                high_ref[rows, cols] = high
                low_ref[rows, cols] = low

    total = None
    for k in range(2):
        high, low = split(down_ref[k])
        rows = slice(OWN * k, OWN * (k + 1))
        part = dot(high, high_ref[rows]) + dot(high, low_ref[rows]) + dot(low, high_ref[rows])
        total = part if total is None else total + part
    mine_ref[...] = total[:, :128]
    theirs_ref[...] = total[:, 128:]


def first_adjoint(core, downgoing, upgoing):
    step = 512
    out = jax.ShapeDtypeStruct((ROWS, 128), F32)
    out_spec = pl.BlockSpec((step, 128), lambda i: (i, 0))
    return pl.pallas_call(
        first_kernel,
        grid=(ROWS // step,),
        in_specs=[
            SMEM,
            pl.BlockSpec((2, step, OWN), lambda i: (0, i, 0)),
            pl.BlockSpec((2, OWN, 128), lambda i: (0, 0, 0)),
        ],
        out_specs=(out_spec, out_spec),
        out_shape=(out, out),
        scratch_shapes=[pltpu.VMEM((2 * OWN, 256), BF16), pltpu.VMEM((2 * OWN, 256), BF16)],
        compiler_params=PARAMS,
        name="first_adjoint",
    )(core, downgoing, upgoing)


def forward_step(piece, own_ref, other_ref, image_ref, keep):
    total = None
    for k, field in enumerate((piece, turn(piece))):
        high, low = split(field.T)
        both = jnp.concatenate([high, low], axis=0)
        blocks = []
        for j, ref in enumerate((own_ref, other_ref)):
            down_high, down_low = split(ref[k])
            keep(k, j, down_high, down_low)
            wide = dot(both, down_high)
            blocks.append(wide[:128] + wide[128:] + dot(high, down_low))
        part = jnp.concatenate(blocks, axis=1)
        total = part if total is None else total + part
    return total


def normal_kernel(g_ref, own_ref, other_ref, q_ref, image_out_ref, high_ref, low_ref, image_ref, w_ref):
    i = pl.program_id(0)

    @pl.when(i < STEPS)
    def _():
        rows = pl.ds(pl.multiple_of(i * STEP, STEP), STEP)

        def keep(k, j, high, low):
            cols = slice(2 * OWN * k + OWN * j, 2 * OWN * k + OWN * (j + 1))
            high_ref[rows, cols] = high
            low_ref[rows, cols] = low

        part = forward_step(g_ref[rows], own_ref, other_ref, image_ref, keep)

        @pl.when(i == 0)
        def _():
            image_ref[...] = part

        @pl.when(i > 0)
        def _():
            image_ref[...] += part

    @pl.when(i == STEPS)
    def _():
        image = image_ref[...].T
        image_out_ref[...] = image
        for rows, field in ((slice(0, 512), image), (slice(512, 1024), -turn(image))):
            high, low = split(field)
            w_ref[rows, :128] = high
            w_ref[rows, 128:] = low

    @pl.when(i >= STEPS)
    def _():
        rows = pl.ds(pl.multiple_of((i - STEPS) * STEP, STEP), STEP)
        wide = dot(high_ref[rows], w_ref[...])
        q_ref[...] = wide[:, :128] + wide[:, 128:] + dot(low_ref[rows], w_ref[:, :128])


def normal(g, own, other):
    down = pl.BlockSpec((2, STEP, OWN), lambda i: (0, jnp.minimum(i, STEPS - 1), 0))
    return pl.pallas_call(
        normal_kernel,
        grid=(2 * STEPS,),
        in_specs=[pl.BlockSpec((ROWS, 128), lambda i: (0, 0)), down, down],
        out_specs=(
            pl.BlockSpec((STEP, 128), lambda i: (jnp.maximum(i - STEPS, 0), 0)),
            pl.BlockSpec((2 * OWN, 128), lambda i: (0, 0)),
        ),
        out_shape=(jax.ShapeDtypeStruct((ROWS, 128), F32), jax.ShapeDtypeStruct((2 * OWN, 128), F32)),
        scratch_shapes=[
            pltpu.VMEM((ROWS, 4 * OWN), BF16),
            pltpu.VMEM((ROWS, 4 * OWN), BF16),
            pltpu.VMEM((128, 2 * OWN), F32),
            pltpu.VMEM((4 * OWN, 256), BF16),
        ],
        compiler_params=PARAMS,
        name="normal_product",
    )(g, own, other)


def second_kernel(place_ref, g_ref, q_ref, own_ref, other_ref, image0_ref, keep_ref, give_ref, row_ref, p_ref, image_ref, scalar_ref):
    i = pl.program_id(0)

    @pl.when(i == 0)
    def _():
        g, q = g_ref[...], q_ref[...]
        gamma0 = jnp.sum(g * g)
        m = jnp.sum(g * q)
        g1 = g - ratio(gamma0, m, 1.0) * q
        gamma1 = jnp.sum(g1 * g1)
        p_ref[...] = g1 + ratio(gamma1, gamma0, 0.0) * g
        scalar_ref[0] = gamma0
        scalar_ref[1] = m
        scalar_ref[2] = gamma1

    rows = pl.ds(pl.multiple_of(i * STEP, STEP), STEP)
    part = forward_step(p_ref[rows], own_ref, other_ref, image_ref, lambda *_: None)

    @pl.when(i == 0)
    def _():
        image_ref[...] = part

    @pl.when(i > 0)
    def _():
        image_ref[...] += part

    @pl.when(i == STEPS - 1)
    def _():
        image = image_ref[...].T
        square = jnp.sum(image * image)
        lane = lax.broadcasted_iota(jnp.int32, row_ref.shape, 2)
        row_ref[...] = jnp.where(
            lane == 0,
            square,
            jnp.where(lane == 1, scalar_ref[0], jnp.where(lane == 2, scalar_ref[1], scalar_ref[2])),
        )
        core, chip = place_ref[0], place_ref[1]
        own_rows = pl.ds(pl.multiple_of(chip * 64 + core * 32, 32), 32)
        other_rows = pl.ds(pl.multiple_of(chip * 64 + (1 - core) * 32, 32), 32)
        keep_ref[:OWN] = image0_ref[:OWN]
        keep_ref[OWN : 2 * OWN] = image[:OWN]
        keep_ref[2 * OWN : 2 * OWN + 32] = g_ref[own_rows]
        keep_ref[2 * OWN + 32 :] = p_ref[own_rows]
        give_ref[:OWN] = image0_ref[OWN:]
        give_ref[OWN : 2 * OWN] = image[OWN:]
        give_ref[2 * OWN : 2 * OWN + 32] = g_ref[other_rows]
        give_ref[2 * OWN + 32 :] = p_ref[other_rows]


def second_forward(place, g, q, own, other, image0):
    down = pl.BlockSpec((2, STEP, OWN), lambda i: (0, i, 0))
    whole = lambda *shape: pl.BlockSpec(shape, lambda i: (0,) * len(shape))
    pack = jax.ShapeDtypeStruct((2 * OWN + 64, 128), F32)
    return pl.pallas_call(
        second_kernel,
        grid=(STEPS,),
        in_specs=[SMEM, whole(ROWS, 128), whole(ROWS, 128), down, down, whole(2 * OWN, 128)],
        out_specs=(whole(*pack.shape), whole(*pack.shape), whole(2 * CHIPS, 8, 128)),
        out_shape=(pack, pack, jax.ShapeDtypeStruct((2 * CHIPS, 8, 128), F32)),
        scratch_shapes=[
            pltpu.VMEM((ROWS, 128), F32),
            pltpu.VMEM((128, 2 * OWN), F32),
            pltpu.SMEM((4,), F32),
        ],
        compiler_params=PARAMS,
        name="second_forward",
    )(place, g, q, own, other, image0)


def last_kernel(place_ref, got_ref, up_ref, keep_ref, take_ref, filt_ref, residual_ref):
    got = got_ref[:, 0, :]
    odd = lax.broadcasted_iota(jnp.int32, got.shape, 0) % 2 == 1
    squares = jnp.sum(jnp.where(odd, 0.0, got), axis=0, keepdims=True), jnp.sum(jnp.where(odd, got, 0.0), axis=0, keepdims=True)
    coefficient = [(squares[c][:, 0:1], got[c : c + 1, 1:2], got[c : c + 1, 2:3], got[c : c + 1, 3:4]) for c in range(2)]
    gamma = coefficient[0][1] + coefficient[1][1]
    alpha0 = gamma / (coefficient[0][2] + coefficient[1][2])
    gamma_new = 0.0
    scales = []
    for square, gamma0, m, gamma1 in coefficient:
        s = alpha0 / ratio(gamma0, m, 1.0)
        scales.append(s)
        gamma_new = gamma_new + s * s * gamma1 + (1.0 - s) * (1.0 - s) * gamma0
    beta = gamma_new / gamma
    norm = 0.0
    shifts = []
    for s, (square, gamma0, m, gamma1) in zip(scales, coefficient):
        e = beta + 1.0 - s - s * ratio(gamma1, gamma0, 0.0)
        shifts.append(e)
        norm = norm + s * s * square + e * e * m
    alpha1 = gamma_new / norm
    for_g = [alpha0 + alpha1 * e for e in shifts]
    for_p = [alpha1 * s for s in scales]

    low = place_ref[0] == 0

    def both(rows):
        mine, theirs = keep_ref[rows], take_ref[rows]
        return jnp.where(low, mine, theirs), jnp.where(low, theirs, mine)

    def combine(first, second):
        columns = [for_g[c] * first[c] + for_p[c] * second[c] for c in range(2)]
        return halves(*columns)

    re, im = combine(both(slice(0, OWN)), both(slice(OWN, 2 * OWN)))
    residual_ref[0] = up_ref[0] - re
    residual_ref[1] = up_ref[1] - im
    re, im = combine(both(slice(2 * OWN, 2 * OWN + 32)), both(slice(2 * OWN + 32, 2 * OWN + 64)))
    filt_ref[:, 0, :] = re
    filt_ref[:, 1, :] = im


def last(place, got, upgoing, keep, take):
    return pl.pallas_call(
        last_kernel,
        in_specs=[SMEM, VMEM, VMEM, VMEM, VMEM],
        out_specs=(VMEM, VMEM),
        out_shape=(jax.ShapeDtypeStruct((32, 2, 128), F32), jax.ShapeDtypeStruct((2, OWN, 128), F32)),
        compiler_params=PARAMS,
        name="last_update",
    )(place, got, upgoing, keep, take)


def exchange(blocks):
    return lax.all_to_all(blocks, ("y", "x"), 0, 0, tiled=True)


def all_sum(partial):
    parts = exchange(partial.reshape(CHIPS, ROWS // CHIPS, 128))
    block = jnp.sum(parts, axis=0)
    return exchange(jnp.broadcast_to(block, parts.shape)).reshape(ROWS, 128)


def on_device(downgoing, upgoing):
    core = lax.axis_index("core").astype(jnp.int32)
    chip = (lax.axis_index("y") * 4 + lax.axis_index("x")).astype(jnp.int32)
    place = jnp.stack([core, chip])
    mine, theirs = first_adjoint(place, downgoing, upgoing)
    theirs = lax.ppermute(theirs, SRC, SWAP)
    other_down, theirs = lax.optimization_barrier((downgoing, theirs))
    other_down = lax.ppermute(other_down, SRC, SWAP)
    g = all_sum(mine + theirs)
    q, image0 = normal(g, downgoing, other_down)
    q = all_sum(q)
    keep, give, row = second_forward(place, g, q, downgoing, other_down, image0)
    take = lax.ppermute(give, SRC, SWAP)
    got = lax.all_to_all(row, SRC, 0, 0, tiled=True)
    return last(place, got, upgoing, keep, take)


def solution(mesh):
    devices = mesh.devices.reshape(mesh.shape["freq"], 8, 4, 2)
    return jax.shard_map(
        on_device,
        mesh=Mesh(devices, ("freq",) + SRC),
        in_specs=(P("freq", None, SRC), P("freq", SRC, None)),
        out_specs=(P(SRC, "freq", None), P("freq", SRC, None)),
        check_vma=False,
    )
```

time: 917 us -> 199 us (0.22)
  waiting for transfers between devices: 463 us -> 13.3 us
  blocking collectives: 379 us -> 126 us
  matrix products: 45.2 us -> 0 us
  Pallas kernels: 0 us -> 32 us
  starting transfers between devices: 0.34 us -> 23.8 us
  between operations: 18.1 us -> 0.7 us
    psum x3 -> x0, blocking collectives: 379 us -> none  [the longest x2 255 us: on_device(): gamma_new = lax.psum(jnp.sum(gradient * gradient), 'src')]
    reduce_scatter x2 -> x0, waiting for transfers between devices: 293 us -> none  [on_device(): lax.psum_scatter(gradient_rows(downgoing, residual), 'src', scatter_dimen...]
    all_gather x2 -> x0, waiting for transfers between devices: 170 us -> none  [on_device(): lax.all_gather(direction, 'src', axis=0, tiled=True)]
    all_to_all x0 -> x4, blocking collectives: none -> 126 us  [exchange(): return lax.all_to_all(blocks, ('y', 'x'), 0, 0, tiled=True)]
    dot_general x16 -> x0, matrix products: 45.2 us -> none  [the longest x8 23.5 us: contract_first(): lax.dot_general(a, b, (((0,), (0,)), ((), ())), precision=HI, preferred_e...]
    pallas_call x0 -> x4, Pallas kernels: none -> 32 us  [the longest x1 13.4 us: normal(): pl.pallas_call(normal_kernel, grid=(2 * STEPS,), in_specs=[pl.BlockSpec((...]
    ppermute x0 -> x3, starting transfers between devices: none -> 13.4 us  [the longest x1 8.78 us: on_device(): theirs = lax.ppermute(theirs, SRC, SWAP)]
    all_to_all x0 -> x1, starting transfers between devices: none -> 10.3 us  [on_device(): got = lax.all_to_all(row, SRC, 0, 0, tiled=True)]
  transfers between devices with their start and end apart: 4 -> 4, of which waited for: 4 -> 3; matrix products, arithmetic and copies ran while one was open for 0% -> 1% of each run, Pallas kernels for 0% -> 0%
where the time goes in v2:
time: 199 us; the launch traced here: 198 us
  blocking collectives  126 us (63%)
  Pallas kernels  32 us (16%)
  starting transfers between devices  23.8 us (12%)
  waiting for transfers between devices  13.3 us (7%)
  other arithmetic  2.12 us (1%)
    all_to_all x4, blocking collectives, exchange(): return lax.all_to_all(blocks, ('y', 'x'), 0, 0, tiled=True)  126 us
    pallas_call x1, Pallas kernels, normal(): pl.pallas_call(normal_kernel, grid=(2 * STEPS,), in_specs=[pl.BlockSpec((...  13.4 us
    pallas_call x1, Pallas kernels, second_forward(): pl.pallas_call(second_kernel, grid=(STEPS,), in_specs=[SMEM, whole(ROWS,...  10.6 us
    all_to_all x1, starting transfers between devices, on_device(): got = lax.all_to_all(row, SRC, 0, 0, tiled=True)  10.3 us
    all_to_all x1, waiting for transfers between devices, on_device(): got = lax.all_to_all(row, SRC, 0, 0, tiled=True)  9.39 us
    ppermute x1, starting transfers between devices, on_device(): theirs = lax.ppermute(theirs, SRC, SWAP)  8.78 us
    pallas_call x1, Pallas kernels, first_adjoint(): pl.pallas_call(first_kernel, grid=(ROWS // step,), in_specs=[SMEM, pl.Blo...  5.57 us
  transfers between devices with their start and end apart: 4, of which 3 were waited for; matrix products, arithmetic and copies ran while one was open for 1% of the time, Pallas kernels for 0%

profile of v2, /device:TPU:1, one launch (start us, length us, event | category | flops | bytes accessed | tf_op | source)
XLA Modules:
  0.0 198.3 jit_solution(16692430574105589483)
XLA Ops:
  0.6 0.7 pad_add_fusion.core_ref.place_ref
  1.3 5.6 %first_adjoint.1 = (f32[2048,128]{1,0:T(8,128)}, f32[2048,128]{1,0:T(8,128)}) custom-call(s32[2]{0:T(128)} %pad_add_fusion.core_ref.place_ref, f32[2,2048,256]{2,1,0:T(8,128)} %own_ref.3, f32[2,256,128]{2,1,0:T(8,128)} %up_ref.3), custom_call_target="tpu_custom_call" | custom-call | tf_op jit(solution)/shard_map/first_adjoint/pallas_call | solution.py:78
  6.9 8.8 %collective-permute-start = (f32[2048,128]{1,0:T(8,128)}, f32[2048,128]{1,0:T(8,128)S(1)}, u32[]{:S(2)}, u32[]{:S(2)}) collective-permute-start(f32[2048,128]{1,0:T(8,128)} %get-tuple-element.12), channel_id=1, source_target_pairs={{0,1},{1,0},{2,3},{3,2},{4,5},{5,4},{6,7},{7,6},{8,9},{9,8},{10,11... | collective-permute-start | bytes 3145736 | tf_op jit(solution)/shard_map/ppermute | solution.py:307
  15.6 2.5 %collective-permute-done = f32[2048,128]{1,0:T(8,128)S(1)} collective-permute-done((f32[2048,128]{1,0:T(8,128)}, f32[2048,128]{1,0:T(8,128)S(1)}, u32[]{:S(2)}, u32[]{:S(2)}) %collective-permute-start) | collective-permute-done | bytes 1048608 | tf_op jit(solution)/shard_map/ppermute | solution.py:307
  18.1 2.3 %collective-permute-start.1 = (f32[2,2048,256]{2,1,0:T(8,128)}, f32[2,2048,256]{2,1,0:T(8,128)}, u32[]{:S(2)}, u32[]{:S(2)}) collective-permute-start(f32[2,2048,256]{2,1,0:T(8,128)} %own_ref.3), channel_id=1, source_target_pairs={{0,1},{1,0},{2,3},{3,2},{4,5},{5,4},{6,7},{7,6},{8,9},{9,8},{10,11... | collective-permute-start | bytes 12582920 | tf_op jit(solution)/shard_map/ppermute | solution.py:309
  20.4 1.3 add.7
  21.7 31.2 %all_to_all.25 = f32[32,64,128]{2,1,0:T(8,128)S(1)} all-to-all(f32[32,64,128]{2,1,0:T(8,128)S(1)} %bitcast.8), channel_id=1, replica_groups=mesh['freq'=8,'y'=8,'x'=4,'core'=2] {'y','x'}, dimensions={0} | all-to-all | bytes 2097152 | tf_op jit(solution)/shard_map/all_to_all | solution.py:293
  52.9 0.1 reduce_sum.18
  53.0 0.1 broadcast_in_dim.6
  53.1 31.4 %all_to_all.26 = f32[32,64,128]{2,1,0:T(8,128)} all-to-all(f32[32,64,128]{2,1,0:T(8,128)S(1)} %broadcast_in_dim.6), channel_id=1, replica_groups=mesh['freq'=8,'y'=8,'x'=4,'core'=2] {'y','x'}, dimensions={0} | all-to-all | bytes 2097152 | tf_op jit(solution)/shard_map/all_to_all | solution.py:293
  84.5 0.0 collective-permute-done.1.other_ref
  84.5 13.4 %normal_product.1 = (f32[2048,128]{1,0:T(8,128)}, f32[512,128]{1,0:T(8,128)}) custom-call(f32[2048,128]{1,0:T(8,128)} %bitcast.6, f32[2,2048,256]{2,1,0:T(8,128)} %own_ref.3, f32[2,2048,256]{2,1,0:T(8,128)} %collective-permute-done.1.other_ref), custom_call_target="tpu_custom_call" | custom-call | tf_op jit(solution)/shard_map/normal_product/pallas_call | solution.py:150
  97.9 31.3 %all_to_all.27 = f32[32,64,128]{2,1,0:T(8,128)S(1)} all-to-all(f32[32,64,128]{2,1,0:T(8,128)} %bitcast.10), channel_id=1, replica_groups=mesh['freq'=8,'y'=8,'x'=4,'core'=2] {'y','x'}, dimensions={0} | all-to-all | bytes 2097152 | tf_op jit(solution)/shard_map/all_to_all | solution.py:293
  129.3 0.1 reduce_sum.19
  129.3 0.1 broadcast_in_dim.7
  129.5 31.7 %all_to_all.28 = f32[32,64,128]{2,1,0:T(8,128)} all-to-all(f32[32,64,128]{2,1,0:T(8,128)S(1)} %broadcast_in_dim.7), channel_id=1, replica_groups=mesh['freq'=8,'y'=8,'x'=4,'core'=2] {'y','x'}, dimensions={0} | all-to-all | bytes 2097152 | tf_op jit(solution)/shard_map/all_to_all | solution.py:293
  161.1 10.6 %second_forward.1 = (f32[576,128]{1,0:T(8,128)}, f32[576,128]{1,0:T(8,128)}, f32[64,8,128]{2,1,0:T(8,128)}) custom-call(s32[2]{0:T(128)} %pad_add_fusion.core_ref.place_ref, f32[2048,128]{1,0:T(8,128)} %bitcast.7, f32[2048,128]{1,0:T(8,128)} %bitcast.9, f32[2,2048,256]{2,1,0:T(8,128)} %own_ref.3, f32[2,2048,256]{2,1,0:T(8,128)} %collective-permute-done.1.other_ref, ...), custom_call_target="tpu_custom_call" | custom-call | tf_op jit(solution)/shard_map/second_forward/pallas_call | solution.py:223
  171.7 10.3 %all-to-all-start.4 = ((f32[64,8,128]{2,1,0:T(8,128)}), f32[64,8,128]{2,1,0:T(8,128)S(1)}, u32[]{:S(2)}, u32[]{:S(2)}) async-start(f32[64,8,128]{2,1,0:T(8,128)} %get-tuple-element.17), calls=%async_computation.4 | async-start | bytes 524288 | tf_op jit(solution)/shard_map/all_to_all | solution.py:315
  182.1 2.4 %collective-permute-start.2 = (f32[576,128]{1,0:T(8,128)}, f32[576,128]{1,0:T(8,128)S(1)}, u32[]{:S(2)}, u32[]{:S(2)}) collective-permute-start(f32[576,128]{1,0:T(8,128)} %get-tuple-element.19), channel_id=1, source_target_pairs={{0,1},{1,0},{2,3},{3,2},{4,5},{5,4},{6,7},{7,6},{8,9},{9,8},{10,11... | collective-permute-start | bytes 884744 | tf_op jit(solution)/shard_map/ppermute | solution.py:314
  184.4 1.4 collective-permute-done.2.take_ref
  185.8 0.0 copy-start.1
  185.8 9.4 %all-to-all-done.4.got_ref = f32[64,8,128]{2,1,0:T(8,128)S(1)} async-done(((f32[64,8,128]{2,1,0:T(8,128)}), f32[64,8,128]{2,1,0:T(8,128)S(1)}, u32[]{:S(2)}, u32[]{:S(2)}) %all-to-all-start.4) | async-done | bytes 262176 | tf_op jit(solution)/shard_map/all_to_all | solution.py:315
  195.2 0.0 copy-start
  195.2 0.0 copy-done.1
  195.2 0.7 copy-done
  195.9 2.4 %last_update.1 = (f32[32,2,128]{2,1,0:T(2,128)}, f32[2,256,128]{2,1,0:T(8,128)}) custom-call(s32[2]{0:T(128)} %pad_add_fusion.core_ref.place_ref, f32[64,8,128]{2,1,0:T(8,128)} %copy-done, f32[2,256,128]{2,1,0:T(8,128)} %up_ref.3, f32[576,128]{1,0:T(8,128)} %get-tuple-element.18.keep_ref, f32[576,128]{1,0:T(8,128)} %copy-done.1), custom_call_target="tpu_custom_call" | custom-call | tf_op jit(solution)/shard_map/last_update/pallas_call | solution.py:282
Async XLA Ops:
  6.9 11.3 %collective-permute-start = (f32[2048,128]{1,0:T(8,128)}, f32[2048,128]{1,0:T(8,128)S(1)}, u32[]{:S(2)}, u32[]{:S(2)}) collective-permute-start(f32[2048,128]{1,0:T(8,128)} %get-tuple-element.12), channel_id=1, source_target_pairs={{0,1},{1,0},{2,3},{3,2},{4,5},{5,4},{6,7},{7,6},{8,9},{9,8},{10,11... | collective-permute-start | bytes 3145736 | tf_op jit(solution)/shard_map/ppermute | solution.py:307
  18.1 66.4 %collective-permute-start.1 = (f32[2,2048,256]{2,1,0:T(8,128)}, f32[2,2048,256]{2,1,0:T(8,128)}, u32[]{:S(2)}, u32[]{:S(2)}) collective-permute-start(f32[2,2048,256]{2,1,0:T(8,128)} %own_ref.3), channel_id=1, source_target_pairs={{0,1},{1,0},{2,3},{3,2},{4,5},{5,4},{6,7},{7,6},{8,9},{9,8},{10,11... | collective-permute-start | bytes 12582920 | tf_op jit(solution)/shard_map/ppermute | solution.py:309
  171.7 23.5 %all-to-all-start.4 = ((f32[64,8,128]{2,1,0:T(8,128)}), f32[64,8,128]{2,1,0:T(8,128)S(1)}, u32[]{:S(2)}, u32[]{:S(2)}) async-start(f32[64,8,128]{2,1,0:T(8,128)} %get-tuple-element.17), calls=%async_computation.4 | async-start | bytes 524288 | tf_op jit(solution)/shard_map/all_to_all | solution.py:315
  182.1 3.8 %collective-permute-start.2 = (f32[576,128]{1,0:T(8,128)}, f32[576,128]{1,0:T(8,128)S(1)}, u32[]{:S(2)}, u32[]{:S(2)}) collective-permute-start(f32[576,128]{1,0:T(8,128)} %get-tuple-element.19), channel_id=1, source_target_pairs={{0,1},{1,0},{2,3},{3,2},{4,5},{5,4},{6,7},{7,6},{8,9},{9,8},{10,11... | collective-permute-start | bytes 884744 | tf_op jit(solution)/shard_map/ppermute | solution.py:314
  185.8 9.4 %copy-start.1 = (f32[576,128]{1,0:T(8,128)}, f32[576,128]{1,0:T(8,128)S(1)}, u32[]{:S(2)}) copy-start(f32[576,128]{1,0:T(8,128)S(1)} %collective-permute-done.2.take_ref) | copy-start | bytes 884740
  195.2 0.7 copy-start

commit v3 on v0

v3 whole, which is shorter than its diff:
```python
import jax
import jax.numpy as jnp
from jax import lax
from jax.experimental import pallas as pl
from jax.experimental.pallas import tpu as pltpu
from jax.sharding import Mesh, PartitionSpec as P

SRC = ("y", "x", "core")
CHIPS = 32
ROWS = 2048
OWN = 256
STEP = 512
STEPS = ROWS // STEP
SWAP = [(i, i ^ 1) for i in range(2 * CHIPS)]
VMEM = pl.BlockSpec(memory_space=pltpu.VMEM)
F32 = jnp.float32
BF16 = jnp.bfloat16


def dot(a, b):
    return jnp.dot(a, b, preferred_element_type=F32)


def split(x):
    high = x.astype(BF16)
    return high, (x - high.astype(F32)).astype(BF16)


def lanes(x):
    return lax.broadcasted_iota(jnp.int32, x.shape, x.ndim - 1) < 64


def turn(z):
    swapped = pltpu.roll(z, 64, 1)
    return jnp.where(lanes(z), -swapped, swapped)


def halves(re, im):
    first = lanes(re)
    return jnp.where(first, re, pltpu.roll(im, 64, 1)), jnp.where(first, pltpu.roll(re, 64, 1), im)


def ratio(a, b, other):
    good = b > 0
    return jnp.where(good, a / jnp.where(good, b, 1.0), other)


def whole_rows(ref, i):
    blocks = [ref[:, y].reshape(STEP // 2, 128) for y in (2 * i, 2 * i + 1)]
    return jnp.concatenate(blocks, axis=0)


def put_rows(ref, i, value):
    for k in range(2):
        ref[:, 2 * i + k] = value[k * STEP // 2 : (k + 1) * STEP // 2].reshape(4, 64, 128)


def first_kernel(down_hbm, up_ref, mine_ref, theirs_ref, down_ref, high_ref, low_ref, sem):
    copies = []
    for i in range(STEPS):
        rows = pl.ds(i * STEP, STEP)
        copies.append(pltpu.make_async_copy(down_hbm.at[:, rows], down_ref.at[:, rows], sem.at[i]))
        copies[-1].start()
    lower, upper = halves(up_ref[0], up_ref[1])
    swap = lax.axis_index("core") == 1
    for k, half in enumerate((jnp.where(swap, upper, lower), jnp.where(swap, lower, upper))):
        cols = slice(128 * k, 128 * k + 128)
        for rows, field in ((slice(0, OWN), half), (slice(OWN, 2 * OWN), -turn(half))):
            high_ref[rows, cols], low_ref[rows, cols] = split(field)
    for i in range(STEPS):
        copies[i].wait()
        total = None
        for k in range(2):
            high, low = split(down_ref[k, i * STEP : (i + 1) * STEP])
            rows = slice(OWN * k, OWN * (k + 1))
            part = dot(high, high_ref[rows]) + dot(high, low_ref[rows]) + dot(low, high_ref[rows])
            total = part if total is None else total + part
        put_rows(mine_ref, i, total[:, :128])
        put_rows(theirs_ref, i, total[:, 128:])


def first_adjoint(downgoing, upgoing):
    out = jax.ShapeDtypeStruct((4, 8, 64, 128), F32)
    return pl.pallas_call(
        first_kernel,
        in_specs=[pl.BlockSpec(memory_space=pl.ANY), VMEM],
        out_specs=(VMEM, VMEM, VMEM),
        out_shape=(out, out, jax.ShapeDtypeStruct(downgoing.shape, F32)),
        scratch_shapes=[
            pltpu.VMEM((2 * OWN, 256), BF16),
            pltpu.VMEM((2 * OWN, 256), BF16),
            pltpu.SemaphoreType.DMA((STEPS,)),
        ],
        compiler_params=pltpu.CompilerParams(vmem_limit_bytes=16 * 2**20),
        name="first_adjoint",
    )(downgoing, upgoing)


def forward_step(piece, own_ref, other_ref, rows, keep):
    total = None
    for k, field in enumerate((piece, turn(piece))):
        high, low = split(field.T)
        both = jnp.concatenate([high, low], axis=0)
        blocks = []
        for j, ref in enumerate((own_ref, other_ref)):
            down_high, down_low = split(ref[k, rows])
            keep(slice(2 * OWN * k + OWN * j, 2 * OWN * k + OWN * (j + 1)), down_high, down_low)
            wide = dot(both, down_high)
            blocks.append(wide[:128] + wide[128:] + dot(high, down_low))
        part = jnp.concatenate(blocks, axis=1)
        total = part if total is None else total + part
    return total


def normal_kernel(g_ref, own_ref, other_ref, q_ref, image_ref, high_ref, low_ref, w_ref):
    total = None
    for i in range(STEPS):
        rows = slice(i * STEP, (i + 1) * STEP)

        def keep(cols, high, low):
            high_ref[rows, cols] = high
            low_ref[rows, cols] = low

        part = forward_step(whole_rows(g_ref, i), own_ref, other_ref, rows, keep)
        total = part if total is None else total + part
    image = total.T
    image_ref[...] = image
    for rows, field in ((slice(0, 512), image), (slice(512, 1024), -turn(image))):
        w_ref[rows, :128], w_ref[rows, 128:] = split(field)
    for i in range(STEPS):
        rows = slice(i * STEP, (i + 1) * STEP)
        wide = dot(high_ref[rows], w_ref[...])
        put_rows(q_ref, i, wide[:, :128] + wide[:, 128:] + dot(low_ref[rows], w_ref[:, :128]))


def normal(g, own, other):
    return pl.pallas_call(
        normal_kernel,
        in_specs=[VMEM, VMEM, VMEM],
        out_specs=(VMEM, VMEM),
        out_shape=(jax.ShapeDtypeStruct(g.shape, F32), jax.ShapeDtypeStruct((2 * OWN, 128), F32)),
        scratch_shapes=[
            pltpu.VMEM((ROWS, 4 * OWN), BF16),
            pltpu.VMEM((ROWS, 4 * OWN), BF16),
            pltpu.VMEM((4 * OWN, 256), BF16),
        ],
        compiler_params=pltpu.CompilerParams(vmem_limit_bytes=40 * 2**20),
        name="normal_product",
    )(g, own, other)


def second_kernel(g_ref, q_ref, own_ref, other_ref, image0_ref, keep_ref, give_ref, row_ref, p_ref):
    g, q = g_ref[...], q_ref[...]
    gamma0 = jnp.sum(g * g)
    m = jnp.sum(g * q)
    g1 = g - ratio(gamma0, m, 1.0) * q
    gamma1 = jnp.sum(g1 * g1)
    p_ref[...] = g1 + ratio(gamma1, gamma0, 0.0) * g

    total = None
    for i in range(STEPS):
        rows = slice(i * STEP, (i + 1) * STEP)
        part = forward_step(whole_rows(p_ref, i), own_ref, other_ref, rows, lambda *_: None)
        total = part if total is None else total + part
    image = total.T
    square = jnp.sum(image * image)
    lane = lax.broadcasted_iota(jnp.int32, row_ref.shape, 2)
    row_ref[...] = jnp.where(
        lane == 0, square, jnp.where(lane == 1, gamma0, jnp.where(lane == 2, m, gamma1))
    )
    x, y, core = lax.axis_index("x"), lax.axis_index("y"), lax.axis_index("core")
    own_rows = pl.ds(pl.multiple_of(core * 32, 32), 32)
    other_rows = pl.ds(pl.multiple_of((1 - core) * 32, 32), 32)
    for ref, sources, receivers in ((keep_ref, slice(0, OWN), own_rows), (give_ref, slice(OWN, 2 * OWN), other_rows)):
        ref[:OWN] = image0_ref[sources]
        ref[OWN : 2 * OWN] = image[sources]
        ref[2 * OWN : 2 * OWN + 32] = g_ref[x, y, receivers]
        ref[2 * OWN + 32 :] = p_ref[x, y, receivers]


def second_forward(g, q, own, other, image0):
    pack = jax.ShapeDtypeStruct((2 * OWN + 64, 128), F32)
    return pl.pallas_call(
        second_kernel,
        in_specs=[VMEM] * 5,
        out_specs=(VMEM,) * 3,
        out_shape=(pack, pack, jax.ShapeDtypeStruct((2 * CHIPS, 1, 128), F32)),
        scratch_shapes=[pltpu.VMEM(g.shape, F32)],
        compiler_params=pltpu.CompilerParams(vmem_limit_bytes=40 * 2**20),
        name="second_forward",
    )(g, q, own, other, image0)


def last_kernel(got_ref, up_ref, keep_ref, take_ref, filt_ref, residual_ref):
    got = got_ref[:, 0, :]
    odd = lax.broadcasted_iota(jnp.int32, got.shape, 0) % 2 == 1
    squares = jnp.sum(jnp.where(odd, 0.0, got), axis=0, keepdims=True), jnp.sum(jnp.where(odd, got, 0.0), axis=0, keepdims=True)
    coefficient = [(squares[c][:, 0:1], got[c : c + 1, 1:2], got[c : c + 1, 2:3], got[c : c + 1, 3:4]) for c in range(2)]
    gamma = coefficient[0][1] + coefficient[1][1]
    alpha0 = gamma / (coefficient[0][2] + coefficient[1][2])
    gamma_new = 0.0
    scales = []
    for square, gamma0, m, gamma1 in coefficient:
        s = alpha0 / ratio(gamma0, m, 1.0)
        scales.append(s)
        gamma_new = gamma_new + s * s * gamma1 + (1.0 - s) * (1.0 - s) * gamma0
    beta = gamma_new / gamma
    norm = 0.0
    shifts = []
    for s, (square, gamma0, m, gamma1) in zip(scales, coefficient):
        e = beta + 1.0 - s - s * ratio(gamma1, gamma0, 0.0)
        shifts.append(e)
        norm = norm + s * s * square + e * e * m
    alpha1 = gamma_new / norm
    for_g = [alpha0 + alpha1 * e for e in shifts]
    for_p = [alpha1 * s for s in scales]

    low = lax.axis_index("core") == 0

    def both(rows):
        mine, theirs = keep_ref[rows], take_ref[rows]
        return jnp.where(low, mine, theirs), jnp.where(low, theirs, mine)

    def combine(first, second):
        columns = [for_g[c] * first[c] + for_p[c] * second[c] for c in range(2)]
        return halves(*columns)

    re, im = combine(both(slice(0, OWN)), both(slice(OWN, 2 * OWN)))
    residual_ref[0] = up_ref[0] - re
    residual_ref[1] = up_ref[1] - im
    re, im = combine(both(slice(2 * OWN, 2 * OWN + 32)), both(slice(2 * OWN + 32, 2 * OWN + 64)))
    filt_ref[:, 0, :] = re
    filt_ref[:, 1, :] = im


def last(got, upgoing, keep, take):
    return pl.pallas_call(
        last_kernel,
        in_specs=[VMEM] * 4,
        out_specs=(VMEM, VMEM),
        out_shape=(jax.ShapeDtypeStruct((32, 2, 128), F32), jax.ShapeDtypeStruct((2, OWN, 128), F32)),
        compiler_params=pltpu.CompilerParams(vmem_limit_bytes=8 * 2**20),
        name="last_update",
    )(got, upgoing, keep, take)


def exchange(blocks, axis):
    return lax.all_to_all(blocks, axis, 0, 0, tiled=True)


def all_sum(partial):
    row = jnp.sum(exchange(partial, "x"), axis=0)
    block = jnp.sum(exchange(row, "y"), axis=0)
    row = exchange(jnp.broadcast_to(block, row.shape), "y")
    return exchange(jnp.broadcast_to(row, partial.shape), "x")


def on_device(downgoing, upgoing):
    mine, theirs, down = first_adjoint(downgoing, upgoing)
    theirs = lax.ppermute(theirs, SRC, SWAP)
    down, theirs = lax.optimization_barrier((down, theirs))
    other_down = lax.ppermute(down, SRC, SWAP)
    g = all_sum(mine + theirs)
    q, image0 = normal(g, down, other_down)
    q = all_sum(q)
    keep, give, row = second_forward(g, q, down, other_down, image0)
    take = lax.ppermute(give, SRC, SWAP)
    got = lax.all_to_all(row, SRC, 0, 0, tiled=True)
    return last(got, upgoing, keep, take)


def solution(mesh):
    devices = mesh.devices.reshape(mesh.shape["freq"], 8, 4, 2)
    return jax.shard_map(
        on_device,
        mesh=Mesh(devices, ("freq",) + SRC),
        in_specs=(P("freq", None, SRC), P("freq", SRC, None)),
        out_specs=(P(SRC, "freq", None), P("freq", SRC, None)),
        check_vma=False,
    )
```

time: 917 us -> 167 us (0.18)
  waiting for transfers between devices: 463 us -> 2.27 us
  blocking collectives: 379 us -> 117 us
  matrix products: 45.2 us -> 0 us
  starting transfers between devices: 0.34 us -> 22 us
  Pallas kernels: 0 us -> 20.9 us
  between operations: 18.1 us -> 0.75 us
    psum x3 -> x0, blocking collectives: 379 us -> none  [the longest x2 255 us: on_device(): gamma_new = lax.psum(jnp.sum(gradient * gradient), 'src')]
    reduce_scatter x2 -> x0, waiting for transfers between devices: 293 us -> none  [on_device(): lax.psum_scatter(gradient_rows(downgoing, residual), 'src', scatter_dimen...]
    all_gather x2 -> x0, waiting for transfers between devices: 170 us -> none  [on_device(): lax.all_gather(direction, 'src', axis=0, tiled=True)]
    all_to_all x0 -> x9, blocking collectives: none -> 117 us  [the longest x8 104 us: exchange(): return lax.all_to_all(blocks, axis, 0, 0, tiled=True)]
    dot_general x16 -> x0, matrix products: 45.2 us -> none  [the longest x8 23.5 us: contract_first(): lax.dot_general(a, b, (((0,), (0,)), ((), ())), precision=HI, preferred_e...]
    ppermute x0 -> x3, starting transfers between devices: none -> 22 us  [the longest x1 10.9 us: on_device(): take = lax.ppermute(give, SRC, SWAP)]
    pallas_call x0 -> x4, Pallas kernels: none -> 20.9 us  [the longest x1 7.77 us: normal(): pl.pallas_call(normal_kernel, in_specs=[VMEM, VMEM, VMEM], out_specs=(VME...]
  transfers between devices with their start and end apart: 4 -> 3, of which waited for: 4 -> 1; matrix products, arithmetic and copies ran while one was open for 0% -> 0% of each run, Pallas kernels for 0% -> 0%
where the time goes in v3:
time: 167 us
  blocking collectives  117 us (70%)
  starting transfers between devices  22 us (13%)
  Pallas kernels  20.9 us (13%)
  local copies, waits for them, and re-layouts  3.39 us (2%)
  waiting for transfers between devices  2.27 us (1%)
    all_to_all x8, blocking collectives, exchange(): return lax.all_to_all(blocks, axis, 0, 0, tiled=True)  104 us
    all_to_all x1, blocking collectives, on_device(): got = lax.all_to_all(row, SRC, 0, 0, tiled=True)  12.7 us
    ppermute x1, starting transfers between devices, on_device(): take = lax.ppermute(give, SRC, SWAP)  10.9 us
    ppermute x1, starting transfers between devices, on_device(): theirs = lax.ppermute(theirs, SRC, SWAP)  8.79 us
    pallas_call x1, Pallas kernels, normal(): pl.pallas_call(normal_kernel, in_specs=[VMEM, VMEM, VMEM], out_specs=(VME...  7.77 us
    pallas_call x1, Pallas kernels, second_forward(): pl.pallas_call(second_kernel, in_specs=[VMEM] * 5, out_specs=(VMEM,) * 3,...  6.54 us
    pallas_call x1, Pallas kernels, first_adjoint(): pl.pallas_call(first_kernel, in_specs=[pl.BlockSpec(memory_space=pl.ANY),...  5.37 us
  transfers between devices with their start and end apart: 3, of which 1 were waited for; matrix products, arithmetic and copies ran while one was open for 0% of the time, Pallas kernels for 0%

profile of v3, /device:TPU:1, one launch (start us, length us, event | category | flops | bytes accessed | tf_op | source)
XLA Modules:
  0.0 166.6 jit_solution(11594692746806820263)
XLA Ops:
  0.6 0.0 copy-start
  0.6 2.2 %copy-done = f32[2,2048,256]{2,1,0:T(8,128)S(1)} copy-done((f32[2,2048,256]{2,1,0:T(8,128)S(1)}, f32[2,2048,256]{2,1,0:T(8,128)}, u32[]{:S(2)}) %copy-start) | copy-done | bytes 4194328
  2.8 0.0 copy-start.1
  2.8 0.9 copy-done.1
  3.8 5.4 %first_adjoint.1 = (f32[4,8,64,128]{3,2,1,0:T(8,128)S(1)}, f32[4,8,64,128]{3,2,1,0:T(8,128)S(1)}, f32[2,2048,256]{2,1,0:T(8,128)}) custom-call(f32[2,2048,256]{2,1,0:T(8,128)S(1)} %copy-done, f32[2,256,128]{2,1,0:T(8,128)S(1)} %copy-done.1), custom_call_target="tpu_custom_call" | custom-call | tf_op jit(solution)/shard_map/first_adjoint/pallas_call | solution.py:84
  9.1 8.8 %collective-permute-start = (f32[4,8,64,128]{3,2,1,0:T(8,128)S(1)}, f32[4,8,64,128]{3,2,1,0:T(8,128)S(1)}, u32[]{:S(2)}, u32[]{:S(2)}) collective-permute-start(f32[4,8,64,128]{3,2,1,0:T(8,128)S(1)} %get-tuple-element.14), channel_id=1, source_target_pairs={{0,1},{1,0},{2,3},{3,2},{4,5},{5,4},{6,7},{7,6},{8,9},{9,8},{10,11... | collective-permute-start | bytes 3145736 | tf_op jit(solution)/shard_map/ppermute | solution.py:260
  17.9 2.3 %collective-permute-done = f32[4,8,64,128]{3,2,1,0:T(8,128)S(1)} collective-permute-done((f32[4,8,64,128]{3,2,1,0:T(8,128)S(1)}, f32[4,8,64,128]{3,2,1,0:T(8,128)S(1)}, u32[]{:S(2)}, u32[]{:S(2)}) %collective-permute-start) | collective-permute-done | bytes 1048608 | tf_op jit(solution)/shard_map/ppermute | solution.py:260
  20.2 2.3 %collective-permute-start.1 = (f32[2,2048,256]{2,1,0:T(8,128)}, f32[2,2048,256]{2,1,0:T(8,128)}, u32[]{:S(2)}, u32[]{:S(2)}) collective-permute-start(f32[2,2048,256]{2,1,0:T(8,128)} %get-tuple-element.16.own_ref), channel_id=1, source_target_pairs={{0,1},{1,0},{2,3},{3,2},{4,5},{5,4},{6,7},{7,6},{8,9},{9,8},{10,11... | collective-permute-start | bytes 12582920 | tf_op jit(solution)/shard_map/ppermute | solution.py:262
  22.5 0.1 add.3
  22.6 17.2 %all_to_all.45 = f32[4,8,64,128]{3,2,1,0:T(8,128)S(1)} all-to-all(f32[4,8,64,128]{3,2,1,0:T(8,128)S(1)} %add.3), channel_id=1, replica_groups=mesh['freq'=8,'y'=8,'x'=4,'core'=2] {'x'}, dimensions={0} | all-to-all | bytes 2097152 | tf_op jit(solution)/shard_map/all_to_all | solution.py:248
  39.9 0.1 reduce_sum.36
  39.9 12.5 %all_to_all.46 = f32[8,64,128]{2,1,0:T(8,128)S(1)} all-to-all(f32[8,64,128]{2,1,0:T(8,128)S(1)} %reduce_sum.36), channel_id=1, replica_groups=mesh['freq'=8,'y'=8,'x'=4,'core'=2] {'y'}, dimensions={0} | all-to-all | bytes 524288 | tf_op jit(solution)/shard_map/all_to_all | solution.py:248
  52.5 12.2 %all_to_all.47 = f32[8,64,128]{2,1,0:T(8,128)S(1)} all-to-all(f32[8,64,128]{2,1,0:T(8,128)S(1)} %broadcast_in_dim.12), channel_id=1, replica_groups=mesh['freq'=8,'y'=8,'x'=4,'core'=2] {'y'}, dimensions={0} | all-to-all | bytes 524288 | tf_op jit(solution)/shard_map/all_to_all | solution.py:248
  64.7 0.1 broadcast_in_dim.13
  64.8 13.8 %all_to_all.48.g_ref = f32[4,8,64,128]{3,2,1,0:T(8,128)S(1)} all-to-all(f32[4,8,64,128]{3,2,1,0:T(8,128)S(1)} %broadcast_in_dim.13), channel_id=1, replica_groups=mesh['freq'=8,'y'=8,'x'=4,'core'=2] {'x'}, dimensions={0} | all-to-all | bytes 2097152 | tf_op jit(solution)/shard_map/all_to_all | solution.py:248
  78.6 0.0 collective-permute-done.1.other_ref
  78.6 7.8 %normal_product.1 = (f32[4,8,64,128]{3,2,1,0:T(8,128)S(1)}, f32[512,128]{1,0:T(8,128)S(1)}) custom-call(f32[4,8,64,128]{3,2,1,0:T(8,128)S(1)} %all_to_all.48.g_ref, f32[2,2048,256]{2,1,0:T(8,128)} %get-tuple-element.16.own_ref, f32[2,2048,256]{2,1,0:T(8,128)} %collective-permute-done.1.other_ref), custom_call_target="tpu_custom_call" | custom-call | tf_op jit(solution)/shard_map/normal_product/pallas_call | solution.py:137
  86.4 12.9 %all_to_all.49 = f32[4,8,64,128]{3,2,1,0:T(8,128)S(1)} all-to-all(f32[4,8,64,128]{3,2,1,0:T(8,128)S(1)} %get-tuple-element.17), channel_id=1, replica_groups=mesh['freq'=8,'y'=8,'x'=4,'core'=2] {'x'}, dimensions={0} | all-to-all | bytes 2097152 | tf_op jit(solution)/shard_map/all_to_all | solution.py:248
  99.3 0.1 reduce_sum.38
  99.3 11.7 %all_to_all.50 = f32[8,64,128]{2,1,0:T(8,128)S(1)} all-to-all(f32[8,64,128]{2,1,0:T(8,128)S(1)} %reduce_sum.38), channel_id=1, replica_groups=mesh['freq'=8,'y'=8,'x'=4,'core'=2] {'y'}, dimensions={0} | all-to-all | bytes 524288 | tf_op jit(solution)/shard_map/all_to_all | solution.py:248
  111.1 11.7 %all_to_all.51 = f32[8,64,128]{2,1,0:T(8,128)S(1)} all-to-all(f32[8,64,128]{2,1,0:T(8,128)S(1)} %broadcast_in_dim.14), channel_id=1, replica_groups=mesh['freq'=8,'y'=8,'x'=4,'core'=2] {'y'}, dimensions={0} | all-to-all | bytes 524288 | tf_op jit(solution)/shard_map/all_to_all | solution.py:248
  122.9 0.1 broadcast_in_dim.15
  123.0 12.2 %all_to_all.52.q_ref = f32[4,8,64,128]{3,2,1,0:T(8,128)S(1)} all-to-all(f32[4,8,64,128]{3,2,1,0:T(8,128)S(1)} %broadcast_in_dim.15), channel_id=1, replica_groups=mesh['freq'=8,'y'=8,'x'=4,'core'=2] {'x'}, dimensions={0} | all-to-all | bytes 2097152 | tf_op jit(solution)/shard_map/all_to_all | solution.py:248
  135.2 0.0 copy-start.2
  135.2 6.5 %second_forward.1 = (f32[576,128]{1,0:T(8,128)S(1)}, f32[576,128]{1,0:T(8,128)S(1)}, f32[64,1,128]{2,1,0:T(1,128)S(1)}) custom-call(f32[4,8,64,128]{3,2,1,0:T(8,128)S(1)} %all_to_all.48.g_ref, f32[4,8,64,128]{3,2,1,0:T(8,128)S(1)} %all_to_all.52.q_ref, f32[2,2048,256]{2,1,0:T(8,128)} %get-tuple-element.16.own_ref, ...), custom_call_target="tpu_custom_call" | custom-call | tf_op jit(solution)/shard_map/second_forward/pallas_call | solution.py:183
  141.7 10.9 %collective-permute-start.2 = (f32[576,128]{1,0:T(8,128)S(1)}, f32[576,128]{1,0:T(8,128)S(1)}, u32[]{:S(2)}, u32[]{:S(2)}) collective-permute-start(f32[576,128]{1,0:T(8,128)S(1)} %get-tuple-element.21), channel_id=1, source_target_pairs={{0,1},{1,0},{2,3},{3,2},{4,5},{5,4},{6,7},{7,6},{8,9},{9,8},{10,11... | collective-permute-start | bytes 884744 | tf_op jit(solution)/shard_map/ppermute | solution.py:267
  152.6 12.7 %all_to_all.53.got_ref = f32[64,1,128]{2,1,0:T(1,128)S(1)} all-to-all(f32[64,1,128]{2,1,0:T(1,128)S(1)} %get-tuple-element.19), channel_id=1, replica_groups=mesh['freq'=8,'y'=8,'x'=4,'core'=2] {'y','x','core'}, dimensions={0} | all-to-all | bytes 65536 | tf_op jit(solution)/shard_map/all_to_all | solution.py:268
  165.4 0.0 collective-permute-done.2.take_ref
  165.4 0.0 copy-done.2
  165.4 1.2 last_update.1
  (4 shorter events, 0.1 us)
Async XLA Ops:
  0.6 2.2 %copy-start = (f32[2,2048,256]{2,1,0:T(8,128)S(1)}, f32[2,2048,256]{2,1,0:T(8,128)}, u32[]{:S(2)}) copy-start(f32[2,2048,256]{2,1,0:T(8,128)} %down_hbm.1) | copy-start | bytes 12582916
  2.8 0.9 copy-start.1
  9.1 11.1 %collective-permute-start = (f32[4,8,64,128]{3,2,1,0:T(8,128)S(1)}, f32[4,8,64,128]{3,2,1,0:T(8,128)S(1)}, u32[]{:S(2)}, u32[]{:S(2)}) collective-permute-start(f32[4,8,64,128]{3,2,1,0:T(8,128)S(1)} %get-tuple-element.14), channel_id=1, source_target_pairs={{0,1},{1,0},{2,3},{3,2},{4,5},{5,4},{6,7},{7,6},{8,9},{9,8},{10,11... | collective-permute-start | bytes 3145736 | tf_op jit(solution)/shard_map/ppermute | solution.py:260
  20.2 58.4 %collective-permute-start.1 = (f32[2,2048,256]{2,1,0:T(8,128)}, f32[2,2048,256]{2,1,0:T(8,128)}, u32[]{:S(2)}, u32[]{:S(2)}) collective-permute-start(f32[2,2048,256]{2,1,0:T(8,128)} %get-tuple-element.16.own_ref), channel_id=1, source_target_pairs={{0,1},{1,0},{2,3},{3,2},{4,5},{5,4},{6,7},{7,6},{8,9},{9,8},{10,11... | collective-permute-start | bytes 12582920 | tf_op jit(solution)/shard_map/ppermute | solution.py:262
  135.2 30.2 %copy-start.2 = (f32[2,256,128]{2,1,0:T(8,128)S(1)}, f32[2,256,128]{2,1,0:T(8,128)}, u32[]{:S(2)}) copy-start(f32[2,256,128]{2,1,0:T(8,128)} %up_ref.3) | copy-start | bytes 786436
  141.7 23.7 %collective-permute-start.2 = (f32[576,128]{1,0:T(8,128)S(1)}, f32[576,128]{1,0:T(8,128)S(1)}, u32[]{:S(2)}, u32[]{:S(2)}) collective-permute-start(f32[576,128]{1,0:T(8,128)S(1)} %get-tuple-element.21), channel_id=1, source_target_pairs={{0,1},{1,0},{2,3},{3,2},{4,5},{5,4},{6,7},{7,6},{8,9},{9,8},{10,11... | collective-permute-start | bytes 884744 | tf_op jit(solution)/shard_map/ppermute | solution.py:267

commit v4 on v3

--- a/solution.py
+++ b/solution.py
@@ -13,8 +13,17 @@
 STEPS = ROWS // STEP
 SWAP = [(i, i ^ 1) for i in range(2 * CHIPS)]
 VMEM = pl.BlockSpec(memory_space=pltpu.VMEM)
+HBM = pl.BlockSpec(memory_space=pltpu.HBM)
 F32 = jnp.float32
 BF16 = jnp.bfloat16
+
+
+def in_vmem(*arrays):
+    return [pltpu.with_memory_space_constraint(a, pltpu.VMEM) for a in arrays]
+
+
+def in_hbm(*arrays):
+    return [pltpu.with_memory_space_constraint(a, pltpu.HBM) for a in arrays]
 
 
 def dot(a, b):
@@ -55,45 +64,45 @@
         ref[:, 2 * i + k] = value[k * STEP // 2 : (k + 1) * STEP // 2].reshape(4, 64, 128)
 
 
-def first_kernel(down_hbm, up_ref, mine_ref, theirs_ref, down_ref, high_ref, low_ref, sem):
-    copies = []
-    for i in range(STEPS):
-        rows = pl.ds(i * STEP, STEP)
-        copies.append(pltpu.make_async_copy(down_hbm.at[:, rows], down_ref.at[:, rows], sem.at[i]))
-        copies[-1].start()
+def first_kernel(down_hbm, up_hbm, mine_ref, theirs_ref, down_ref, up_ref, high_ref, low_ref, sem):
+    field_copy = pltpu.make_async_copy(up_hbm, up_ref, sem.at[0])
+    field_copy.start()
+    down_copy = pltpu.make_async_copy(down_hbm, down_ref, sem.at[1])
+    down_copy.start()
+    field_copy.wait()
     lower, upper = halves(up_ref[0], up_ref[1])
     swap = lax.axis_index("core") == 1
     for k, half in enumerate((jnp.where(swap, upper, lower), jnp.where(swap, lower, upper))):
         cols = slice(128 * k, 128 * k + 128)
         for rows, field in ((slice(0, OWN), half), (slice(OWN, 2 * OWN), -turn(half))):
             high_ref[rows, cols], low_ref[rows, cols] = split(field)
+    down_copy.wait()
+    parts = [split(down_ref[k]) for k in range(2)]
+    high = jnp.concatenate([parts[0][0], parts[1][0]], axis=1)
+    low = jnp.concatenate([parts[0][1], parts[1][1]], axis=1)
+    total = dot(high, high_ref[...]) + dot(high, low_ref[...]) + dot(low, high_ref[...])
     for i in range(STEPS):
-        copies[i].wait()
-        total = None
-        for k in range(2):
-            high, low = split(down_ref[k, i * STEP : (i + 1) * STEP])
-            rows = slice(OWN * k, OWN * (k + 1))
-            part = dot(high, high_ref[rows]) + dot(high, low_ref[rows]) + dot(low, high_ref[rows])
-            total = part if total is None else total + part
-        put_rows(mine_ref, i, total[:, :128])
-        put_rows(theirs_ref, i, total[:, 128:])
+        rows = slice(i * STEP, (i + 1) * STEP)
+        put_rows(mine_ref, i, total[rows, :128])
+        put_rows(theirs_ref, i, total[rows, 128:])
 
 
 def first_adjoint(downgoing, upgoing):
-    out = jax.ShapeDtypeStruct((4, 8, 64, 128), F32)
+    out = pltpu.VMEM((4, 8, 64, 128), F32)
     return pl.pallas_call(
         first_kernel,
-        in_specs=[pl.BlockSpec(memory_space=pl.ANY), VMEM],
+        in_specs=[HBM, HBM],
         out_specs=(VMEM, VMEM, VMEM),
-        out_shape=(out, out, jax.ShapeDtypeStruct(downgoing.shape, F32)),
+        out_shape=(out, out, pltpu.VMEM(downgoing.shape, F32)),
         scratch_shapes=[
+            pltpu.VMEM(upgoing.shape, F32),
             pltpu.VMEM((2 * OWN, 256), BF16),
             pltpu.VMEM((2 * OWN, 256), BF16),
-            pltpu.SemaphoreType.DMA((STEPS,)),
+            pltpu.SemaphoreType.DMA((2,)),
         ],
-        compiler_params=pltpu.CompilerParams(vmem_limit_bytes=16 * 2**20),
+        compiler_params=pltpu.CompilerParams(vmem_limit_bytes=24 * 2**20),
         name="first_adjoint",
-    )(downgoing, upgoing)
+    )(*in_hbm(downgoing, upgoing))
 
 
 def forward_step(piece, own_ref, other_ref, rows, keep):
@@ -138,15 +147,15 @@
         normal_kernel,
         in_specs=[VMEM, VMEM, VMEM],
         out_specs=(VMEM, VMEM),
-        out_shape=(jax.ShapeDtypeStruct(g.shape, F32), jax.ShapeDtypeStruct((2 * OWN, 128), F32)),
+        out_shape=(pltpu.VMEM(g.shape, F32), pltpu.VMEM((2 * OWN, 128), F32)),
         scratch_shapes=[
             pltpu.VMEM((ROWS, 4 * OWN), BF16),
             pltpu.VMEM((ROWS, 4 * OWN), BF16),
             pltpu.VMEM((4 * OWN, 256), BF16),
         ],
-        compiler_params=pltpu.CompilerParams(vmem_limit_bytes=40 * 2**20),
+        compiler_params=pltpu.CompilerParams(vmem_limit_bytes=28 * 2**20),
         name="normal_product",
-    )(g, own, other)
+    )(*in_vmem(g, own, other))
 
 
 def second_kernel(g_ref, q_ref, own_ref, other_ref, image0_ref, keep_ref, give_ref, row_ref, p_ref):
@@ -179,16 +188,16 @@
 
 
 def second_forward(g, q, own, other, image0):
-    pack = jax.ShapeDtypeStruct((2 * OWN + 64, 128), F32)
+    pack = pltpu.VMEM((2 * OWN + 64, 128), F32)
     return pl.pallas_call(
         second_kernel,
         in_specs=[VMEM] * 5,
         out_specs=(VMEM,) * 3,
-        out_shape=(pack, pack, jax.ShapeDtypeStruct((2 * CHIPS, 1, 128), F32)),
+        out_shape=(pack, pack, pltpu.VMEM((2 * CHIPS, 1, 128), F32)),
         scratch_shapes=[pltpu.VMEM(g.shape, F32)],
-        compiler_params=pltpu.CompilerParams(vmem_limit_bytes=40 * 2**20),
+        compiler_params=pltpu.CompilerParams(vmem_limit_bytes=16 * 2**20),
         name="second_forward",
-    )(g, q, own, other, image0)
+    )(*in_vmem(g, q, own, other, image0))
 
 
 def last_kernel(got_ref, up_ref, keep_ref, take_ref, filt_ref, residual_ref):
@@ -239,20 +248,58 @@
         in_specs=[VMEM] * 4,
         out_specs=(VMEM, VMEM),
         out_shape=(jax.ShapeDtypeStruct((32, 2, 128), F32), jax.ShapeDtypeStruct((2, OWN, 128), F32)),
-        compiler_params=pltpu.CompilerParams(vmem_limit_bytes=8 * 2**20),
+        compiler_params=pltpu.CompilerParams(vmem_limit_bytes=12 * 2**20),
         name="last_update",
     )(got, upgoing, keep, take)
 
 
+def small(body, shape, name, *arrays):
+    return pl.pallas_call(
+        body,
+        in_specs=[VMEM] * len(arrays),
+        out_specs=VMEM,
+        out_shape=pltpu.VMEM(shape, F32),
+        compiler_params=pltpu.CompilerParams(vmem_limit_bytes=4 * 2**20),
+        name=name,
+    )(*in_vmem(*arrays))
+
+
+def add_kernel(a_ref, b_ref, out_ref):
+    out_ref[...] = a_ref[...] + b_ref[...]
+
+
+def total(ref):
+    value = ref[0]
+    for k in range(1, ref.shape[0]):
+        value = value + ref[k]
+    return value
+
+
+def sum_kernel(ref, out_ref):
+    out_ref[...] = total(ref)
+
+
+def sum_repeat_kernel(ref, out_ref):
+    value = total(ref)
+    for k in range(out_ref.shape[0]):
+        out_ref[k] = value
+
+
+def repeat_kernel(ref, out_ref):
+    value = ref[...]
+    for k in range(out_ref.shape[0]):
+        out_ref[k] = value
+
+
 def exchange(blocks, axis):
     return lax.all_to_all(blocks, axis, 0, 0, tiled=True)
 
 
 def all_sum(partial):
-    row = jnp.sum(exchange(partial, "x"), axis=0)
-    block = jnp.sum(exchange(row, "y"), axis=0)
-    row = exchange(jnp.broadcast_to(block, row.shape), "y")
-    return exchange(jnp.broadcast_to(row, partial.shape), "x")
+    row = small(sum_kernel, partial.shape[1:], "sum_x", exchange(partial, "x"))
+    row = small(sum_repeat_kernel, row.shape, "sum_y", exchange(row, "y"))
+    whole = small(repeat_kernel, partial.shape, "repeat_x", exchange(row, "y"))
+    return exchange(whole, "x")
 
 
 def on_device(downgoing, upgoing):
@@ -260,7 +307,7 @@
     theirs = lax.ppermute(theirs, SRC, SWAP)
     down, theirs = lax.optimization_barrier((down, theirs))
     other_down = lax.ppermute(down, SRC, SWAP)
-    g = all_sum(mine + theirs)
+    g = all_sum(small(add_kernel, mine.shape, "add_cores", mine, theirs))
     q, image0 = normal(g, down, other_down)
     q = all_sum(q)
     keep, give, row = second_forward(g, q, down, other_down, image0)

time: 167 us -> 156 us (0.934)
  Pallas kernels: 20.9 us -> 13.1 us
  local copies, waits for them, and re-layouts: 3.39 us -> 0.01 us
    pallas_call x1, Pallas kernels: 6.54 us -> 3.02 us  [second_forward(): pl.pallas_call(second_kernel, in_specs=[VMEM] * 5, out_specs=(VMEM,) * 3,...]
    pallas_call x1, Pallas kernels: 7.77 us -> 4.32 us  [normal(): pl.pallas_call(normal_kernel, in_specs=[VMEM, VMEM, VMEM], out_specs=(VME...]
    unnamed x6 -> x2, local copies, waits for them, and re-layouts: 3.13 us -> 0.01 us
    pallas_call x1 -> x8, Pallas kernels: 5.37 us -> 4.5 us  [the longest x1 4.11 us: first_adjoint(): pl.pallas_call(first_kernel, in_specs=[HBM, HBM], out_specs=(VMEM, VMEM,...]
where the time goes in v4:
time: 156 us; the launch traced here: 155 us
  blocking collectives  117 us (75%)
  starting transfers between devices  22 us (14%)
  Pallas kernels  13.1 us (8%)
  waiting for transfers between devices  2.27 us (1%)
    all_to_all x8, blocking collectives, exchange(): return lax.all_to_all(blocks, axis, 0, 0, tiled=True)  104 us
    all_to_all x1, blocking collectives, on_device(): got = lax.all_to_all(row, SRC, 0, 0, tiled=True)  12.7 us
    ppermute x1, starting transfers between devices, on_device(): take = lax.ppermute(give, SRC, SWAP)  10.9 us
    ppermute x1, starting transfers between devices, on_device(): theirs = lax.ppermute(theirs, SRC, SWAP)  8.79 us
    pallas_call x1, Pallas kernels, normal(): pl.pallas_call(normal_kernel, in_specs=[VMEM, VMEM, VMEM], out_specs=(VME...  4.32 us
    pallas_call x1, Pallas kernels, first_adjoint(): pl.pallas_call(first_kernel, in_specs=[HBM, HBM], out_specs=(VMEM, VMEM,...  4.11 us
  transfers between devices with their start and end apart: 3, of which 1 were waited for; matrix products, arithmetic and copies ran while one was open for 0% of the time, Pallas kernels for 0%

profile of v4, /device:TPU:1, one launch (start us, length us, event | category | flops | bytes accessed | tf_op | source)
XLA Modules:
  0.0 155.0 jit_solution(8700200599323865157)
XLA Ops:
  0.6 4.1 %first_adjoint.1 = (f32[4,8,64,128]{3,2,1,0:T(8,128)S(1)}, f32[4,8,64,128]{3,2,1,0:T(8,128)S(1)}, f32[2,2048,256]{2,1,0:T(8,128)S(1)}) custom-call(f32[2,2048,256]{2,1,0:T(8,128)} %down_hbm.1, f32[2,256,128]{2,1,0:T(8,128)} %up_ref.1), custom_call_target="tpu_custom_call" | custom-call | tf_op jit(solution)/shard_map/first_adjoint/pallas_call | solution.py:92
  4.7 8.8 %collective-permute-start = (f32[4,8,64,128]{3,2,1,0:T(8,128)S(1)}, f32[4,8,64,128]{3,2,1,0:T(8,128)S(1)}, u32[]{:S(2)}, u32[]{:S(2)}) collective-permute-start(f32[4,8,64,128]{3,2,1,0:T(8,128)S(1)} %get-tuple-element.14), channel_id=1, source_target_pairs={{0,1},{1,0},{2,3},{3,2},{4,5},{5,4},{6,7},{7,6},{8,9},{9,8},{10,11... | collective-permute-start | bytes 3145736 | tf_op jit(solution)/shard_map/ppermute | solution.py:307
  13.5 2.3 %collective-permute-done.b_ref = f32[4,8,64,128]{3,2,1,0:T(8,128)S(1)} collective-permute-done((f32[4,8,64,128]{3,2,1,0:T(8,128)S(1)}, f32[4,8,64,128]{3,2,1,0:T(8,128)S(1)}, u32[]{:S(2)}, u32[]{:S(2)}) %collective-permute-start) | collective-permute-done | bytes 1048608 | tf_op jit(solution)/shard_map/ppermute | solution.py:307
  15.8 2.3 %collective-permute-start.1 = (f32[2,2048,256]{2,1,0:T(8,128)S(1)}, f32[2,2048,256]{2,1,0:T(8,128)S(1)}, u32[]{:S(2)}, u32[]{:S(2)}) collective-permute-start(f32[2,2048,256]{2,1,0:T(8,128)S(1)} %get-tuple-element.16.own_ref), channel_id=1, source_target_pairs={{0,1},{1,0},{2,3},{3,2},{4,5},{5,4},{6,7},{7,6},{8,9},{9,8},{10,11... | collective-permute-start | bytes 12582920 | tf_op jit(solution)/shard_map/ppermute | solution.py:309
  18.1 0.1 add_cores.1
  18.2 17.2 %all_to_all.45.ref = f32[4,8,64,128]{3,2,1,0:T(8,128)S(1)} all-to-all(f32[4,8,64,128]{3,2,1,0:T(8,128)S(1)} %add_cores.1), channel_id=1, replica_groups=mesh['freq'=8,'y'=8,'x'=4,'core'=2] {'x'}, dimensions={0} | all-to-all | bytes 2097152 | tf_op jit(solution)/shard_map/all_to_all | solution.py:295
  35.5 12.5 %all_to_all.46.ref = f32[8,64,128]{2,1,0:T(8,128)S(1)} all-to-all(f32[8,64,128]{2,1,0:T(8,128)S(1)} %sum_x.2), channel_id=1, replica_groups=mesh['freq'=8,'y'=8,'x'=4,'core'=2] {'y'}, dimensions={0} | all-to-all | bytes 524288 | tf_op jit(solution)/shard_map/all_to_all | solution.py:295
  48.0 12.2 %all_to_all.47.ref = f32[8,64,128]{2,1,0:T(8,128)S(1)} all-to-all(f32[8,64,128]{2,1,0:T(8,128)S(1)} %sum_y.2), channel_id=1, replica_groups=mesh['freq'=8,'y'=8,'x'=4,'core'=2] {'y'}, dimensions={0} | all-to-all | bytes 524288 | tf_op jit(solution)/shard_map/all_to_all | solution.py:295
  60.2 0.1 repeat_x.2
  60.3 13.8 %all_to_all.48.g_ref = f32[4,8,64,128]{3,2,1,0:T(8,128)S(1)} all-to-all(f32[4,8,64,128]{3,2,1,0:T(8,128)S(1)} %repeat_x.2), channel_id=1, replica_groups=mesh['freq'=8,'y'=8,'x'=4,'core'=2] {'x'}, dimensions={0} | all-to-all | bytes 2097152 | tf_op jit(solution)/shard_map/all_to_all | solution.py:295
  74.1 0.0 collective-permute-done.1.other_ref
  74.1 4.3 %normal_product.1 = (f32[4,8,64,128]{3,2,1,0:T(8,128)S(1)}, f32[512,128]{1,0:T(8,128)S(1)}) custom-call(f32[4,8,64,128]{3,2,1,0:T(8,128)S(1)} %all_to_all.48.g_ref, f32[2,2048,256]{2,1,0:T(8,128)S(1)} %get-tuple-element.16.own_ref, f32[2,2048,256]{2,1,0:T(8,128)S(1)} %collective-permute-done.1.other_ref), custom_call_target="tpu_custom_call" | custom-call | tf_op jit(solution)/shard_map/normal_product/pallas_call | solution.py:146
  78.4 12.9 %all_to_all.49.ref = f32[4,8,64,128]{3,2,1,0:T(8,128)S(1)} all-to-all(f32[4,8,64,128]{3,2,1,0:T(8,128)S(1)} %get-tuple-element.17), channel_id=1, replica_groups=mesh['freq'=8,'y'=8,'x'=4,'core'=2] {'x'}, dimensions={0} | all-to-all | bytes 2097152 | tf_op jit(solution)/shard_map/all_to_all | solution.py:295
  91.4 11.7 %all_to_all.50.ref = f32[8,64,128]{2,1,0:T(8,128)S(1)} all-to-all(f32[8,64,128]{2,1,0:T(8,128)S(1)} %sum_x.3), channel_id=1, replica_groups=mesh['freq'=8,'y'=8,'x'=4,'core'=2] {'y'}, dimensions={0} | all-to-all | bytes 524288 | tf_op jit(solution)/shard_map/all_to_all | solution.py:295
  103.1 11.7 %all_to_all.51.ref = f32[8,64,128]{2,1,0:T(8,128)S(1)} all-to-all(f32[8,64,128]{2,1,0:T(8,128)S(1)} %sum_y.3), channel_id=1, replica_groups=mesh['freq'=8,'y'=8,'x'=4,'core'=2] {'y'}, dimensions={0} | all-to-all | bytes 524288 | tf_op jit(solution)/shard_map/all_to_all | solution.py:295
  114.9 0.1 repeat_x.3
  114.9 12.2 %all_to_all.52.q_ref = f32[4,8,64,128]{3,2,1,0:T(8,128)S(1)} all-to-all(f32[4,8,64,128]{3,2,1,0:T(8,128)S(1)} %repeat_x.3), channel_id=1, replica_groups=mesh['freq'=8,'y'=8,'x'=4,'core'=2] {'x'}, dimensions={0} | all-to-all | bytes 2097152 | tf_op jit(solution)/shard_map/all_to_all | solution.py:295
  127.1 0.0 copy-start
  127.1 3.0 %second_forward.1 = (f32[576,128]{1,0:T(8,128)S(1)}, f32[576,128]{1,0:T(8,128)S(1)}, f32[64,1,128]{2,1,0:T(1,128)S(1)}) custom-call(f32[4,8,64,128]{3,2,1,0:T(8,128)S(1)} %all_to_all.48.g_ref, f32[4,8,64,128]{3,2,1,0:T(8,128)S(1)} %all_to_all.52.q_ref, f32[2,2048,256]{2,1,0:T(8,128)S(1)} %get-tuple-element.16.own_ref, ...), custom_call_target="tpu_custom_call" | custom-call | tf_op jit(solution)/shard_map/second_forward/pallas_call | solution.py:192
  130.1 10.9 %collective-permute-start.2 = (f32[576,128]{1,0:T(8,128)S(1)}, f32[576,128]{1,0:T(8,128)S(1)}, u32[]{:S(2)}, u32[]{:S(2)}) collective-permute-start(f32[576,128]{1,0:T(8,128)S(1)} %get-tuple-element.21), channel_id=1, source_target_pairs={{0,1},{1,0},{2,3},{3,2},{4,5},{5,4},{6,7},{7,6},{8,9},{9,8},{10,11... | collective-permute-start | bytes 884744 | tf_op jit(solution)/shard_map/ppermute | solution.py:314
  141.1 12.7 %all_to_all.53.got_ref = f32[64,1,128]{2,1,0:T(1,128)S(1)} all-to-all(f32[64,1,128]{2,1,0:T(1,128)S(1)} %get-tuple-element.19), channel_id=1, replica_groups=mesh['freq'=8,'y'=8,'x'=4,'core'=2] {'y','x','core'}, dimensions={0} | all-to-all | bytes 65536 | tf_op jit(solution)/shard_map/all_to_all | solution.py:315
  153.8 0.0 collective-permute-done.2.take_ref
  153.8 0.0 copy-done
  153.8 1.2 last_update.1
  (4 shorter events, 0.1 us)
Async XLA Ops:
  4.7 11.1 %collective-permute-start = (f32[4,8,64,128]{3,2,1,0:T(8,128)S(1)}, f32[4,8,64,128]{3,2,1,0:T(8,128)S(1)}, u32[]{:S(2)}, u32[]{:S(2)}) collective-permute-start(f32[4,8,64,128]{3,2,1,0:T(8,128)S(1)} %get-tuple-element.14), channel_id=1, source_target_pairs={{0,1},{1,0},{2,3},{3,2},{4,5},{5,4},{6,7},{7,6},{8,9},{9,8},{10,11... | collective-permute-start | bytes 3145736 | tf_op jit(solution)/shard_map/ppermute | solution.py:307
  15.8 58.3 %collective-permute-start.1 = (f32[2,2048,256]{2,1,0:T(8,128)S(1)}, f32[2,2048,256]{2,1,0:T(8,128)S(1)}, u32[]{:S(2)}, u32[]{:S(2)}) collective-permute-start(f32[2,2048,256]{2,1,0:T(8,128)S(1)} %get-tuple-element.16.own_ref), channel_id=1, source_target_pairs={{0,1},{1,0},{2,3},{3,2},{4,5},{5,4},{6,7},{7,6},{8,9},{9,8},{10,11... | collective-permute-start | bytes 12582920 | tf_op jit(solution)/shard_map/ppermute | solution.py:309
  127.1 26.7 %copy-start = (f32[2,256,128]{2,1,0:T(8,128)S(1)}, f32[2,256,128]{2,1,0:T(8,128)}, u32[]{:S(2)}) copy-start(f32[2,256,128]{2,1,0:T(8,128)} %up_ref.1) | copy-start | bytes 786436
  130.1 23.7 %collective-permute-start.2 = (f32[576,128]{1,0:T(8,128)S(1)}, f32[576,128]{1,0:T(8,128)S(1)}, u32[]{:S(2)}, u32[]{:S(2)}) collective-permute-start(f32[576,128]{1,0:T(8,128)S(1)} %get-tuple-element.21), channel_id=1, source_target_pairs={{0,1},{1,0},{2,3},{3,2},{4,5},{5,4},{6,7},{7,6},{8,9},{9,8},{10,11... | collective-permute-start | bytes 884744 | tf_op jit(solution)/shard_map/ppermute | solution.py:314

commit v5 on v4

--- a/solution.py
+++ b/solution.py
@@ -5,7 +5,8 @@
 from jax.experimental.pallas import tpu as pltpu
 from jax.sharding import Mesh, PartitionSpec as P
 
-SRC = ("y", "x", "core")
+SRC = ("y_high", "y_low", "x", "core")
+NEAR = ("y_low", "x")
 CHIPS = 32
 ROWS = 2048
 OWN = 256
@@ -55,13 +56,11 @@
 
 
 def whole_rows(ref, i):
-    blocks = [ref[:, y].reshape(STEP // 2, 128) for y in (2 * i, 2 * i + 1)]
-    return jnp.concatenate(blocks, axis=0)
+    return ref[:, i].reshape(STEP, 128)
 
 
 def put_rows(ref, i, value):
-    for k in range(2):
-        ref[:, 2 * i + k] = value[k * STEP // 2 : (k + 1) * STEP // 2].reshape(4, 64, 128)
+    ref[:, i] = value.reshape(8, 64, 128)
 
 
 def first_kernel(down_hbm, up_hbm, mine_ref, theirs_ref, down_ref, up_ref, high_ref, low_ref, sem):
@@ -88,7 +87,7 @@
 
 
 def first_adjoint(downgoing, upgoing):
-    out = pltpu.VMEM((4, 8, 64, 128), F32)
+    out = pltpu.VMEM((8, 4, 64, 128), F32)
     return pl.pallas_call(
         first_kernel,
         in_specs=[HBM, HBM],
@@ -177,14 +176,15 @@
     row_ref[...] = jnp.where(
         lane == 0, square, jnp.where(lane == 1, gamma0, jnp.where(lane == 2, m, gamma1))
     )
-    x, y, core = lax.axis_index("x"), lax.axis_index("y"), lax.axis_index("core")
+    near = lax.axis_index("y_low") * 4 + lax.axis_index("x")
+    far, core = lax.axis_index("y_high"), lax.axis_index("core")
     own_rows = pl.ds(pl.multiple_of(core * 32, 32), 32)
     other_rows = pl.ds(pl.multiple_of((1 - core) * 32, 32), 32)
     for ref, sources, receivers in ((keep_ref, slice(0, OWN), own_rows), (give_ref, slice(OWN, 2 * OWN), other_rows)):
         ref[:OWN] = image0_ref[sources]
         ref[OWN : 2 * OWN] = image[sources]
-        ref[2 * OWN : 2 * OWN + 32] = g_ref[x, y, receivers]
-        ref[2 * OWN + 32 :] = p_ref[x, y, receivers]
+        ref[2 * OWN : 2 * OWN + 32] = g_ref[near, far, receivers]
+        ref[2 * OWN + 32 :] = p_ref[near, far, receivers]
 
 
 def second_forward(g, q, own, other, image0):
@@ -296,10 +296,10 @@
 
 
 def all_sum(partial):
-    row = small(sum_kernel, partial.shape[1:], "sum_x", exchange(partial, "x"))
-    row = small(sum_repeat_kernel, row.shape, "sum_y", exchange(row, "y"))
-    whole = small(repeat_kernel, partial.shape, "repeat_x", exchange(row, "y"))
-    return exchange(whole, "x")
+    row = small(sum_kernel, partial.shape[1:], "sum_near", exchange(partial, NEAR))
+    row = small(sum_repeat_kernel, row.shape, "sum_far", exchange(row, "y_high"))
+    whole = small(repeat_kernel, partial.shape, "repeat_near", exchange(row, "y_high"))
+    return exchange(whole, NEAR)
 
 
 def on_device(downgoing, upgoing):
@@ -317,7 +317,7 @@
 
 
 def solution(mesh):
-    devices = mesh.devices.reshape(mesh.shape["freq"], 8, 4, 2)
+    devices = mesh.devices.reshape(mesh.shape["freq"], 4, 2, 4, 2)
     return jax.shard_map(
         on_device,
         mesh=Mesh(devices, ("freq",) + SRC),

time: 156 us -> 151 us (0.968)
  blocking collectives: 117 us -> 111 us
    all_to_all x8, blocking collectives: 104 us -> 98.2 us  [exchange(): return lax.all_to_all(blocks, axis, 0, 0, tiled=True)]
where the time goes in v5:
time: 151 us
  blocking collectives  111 us (74%)
  starting transfers between devices  23.5 us (16%)
  Pallas kernels  13 us (9%)
  waiting for transfers between devices  2.27 us (2%)
    all_to_all x8, blocking collectives, exchange(): return lax.all_to_all(blocks, axis, 0, 0, tiled=True)  98.2 us
    all_to_all x1, blocking collectives, on_device(): got = lax.all_to_all(row, SRC, 0, 0, tiled=True)  12.7 us
    ppermute x1, starting transfers between devices, on_device(): take = lax.ppermute(give, SRC, SWAP)  12.5 us
    ppermute x1, starting transfers between devices, on_device(): theirs = lax.ppermute(theirs, SRC, SWAP)  8.79 us
    pallas_call x1, Pallas kernels, normal(): pl.pallas_call(normal_kernel, in_specs=[VMEM, VMEM, VMEM], out_specs=(VME...  4.32 us
    pallas_call x1, Pallas kernels, first_adjoint(): pl.pallas_call(first_kernel, in_specs=[HBM, HBM], out_specs=(VMEM, VMEM,...  4.11 us
    pallas_call x1, Pallas kernels, second_forward(): pl.pallas_call(second_kernel, in_specs=[VMEM] * 5, out_specs=(VMEM,) * 3,...  3.03 us
  transfers between devices with their start and end apart: 3, of which 1 were waited for; matrix products, arithmetic and copies ran while one was open for 0% of the time, Pallas kernels for 0%

profile of v5, /device:TPU:1, one launch (start us, length us, event | category | flops | bytes accessed | tf_op | source)
XLA Modules:
  0.0 150.5 jit_solution(4244023061987865328)
XLA Ops:
  0.6 4.1 %first_adjoint.1 = (f32[8,4,64,128]{3,2,1,0:T(8,128)S(1)}, f32[8,4,64,128]{3,2,1,0:T(8,128)S(1)}, f32[2,2048,256]{2,1,0:T(8,128)S(1)}) custom-call(f32[2,2048,256]{2,1,0:T(8,128)} %down_hbm.1, f32[2,256,128]{2,1,0:T(8,128)} %up_ref.1), custom_call_target="tpu_custom_call" | custom-call | tf_op jit(solution)/shard_map/first_adjoint/pallas_call | solution.py:91
  4.7 8.8 %collective-permute-start = (f32[8,4,64,128]{3,2,1,0:T(8,128)S(1)}, f32[8,4,64,128]{3,2,1,0:T(8,128)S(1)}, u32[]{:S(2)}, u32[]{:S(2)}) collective-permute-start(f32[8,4,64,128]{3,2,1,0:T(8,128)S(1)} %get-tuple-element.14), channel_id=1, source_target_pairs={{0,1},{1,0},{2,3},{3,2},{4,5},{5,4},{6,7},{7,6},{8,9},{9,8},{10,11... | collective-permute-start | bytes 3145736 | tf_op jit(solution)/shard_map/ppermute | solution.py:307
  13.5 2.3 %collective-permute-done.b_ref = f32[8,4,64,128]{3,2,1,0:T(8,128)S(1)} collective-permute-done((f32[8,4,64,128]{3,2,1,0:T(8,128)S(1)}, f32[8,4,64,128]{3,2,1,0:T(8,128)S(1)}, u32[]{:S(2)}, u32[]{:S(2)}) %collective-permute-start) | collective-permute-done | bytes 1048608 | tf_op jit(solution)/shard_map/ppermute | solution.py:307
  15.8 2.3 %collective-permute-start.1 = (f32[2,2048,256]{2,1,0:T(8,128)S(1)}, f32[2,2048,256]{2,1,0:T(8,128)S(1)}, u32[]{:S(2)}, u32[]{:S(2)}) collective-permute-start(f32[2,2048,256]{2,1,0:T(8,128)S(1)} %get-tuple-element.16.own_ref), channel_id=1, source_target_pairs={{0,1},{1,0},{2,3},{3,2},{4,5},{5,4},{6,7},{7,6},{8,9},{9,8},{10,11... | collective-permute-start | bytes 12582920 | tf_op jit(solution)/shard_map/ppermute | solution.py:309
  18.1 0.1 add_cores.1
  18.2 17.1 %all_to_all.45.ref = f32[8,4,64,128]{3,2,1,0:T(8,128)S(1)} all-to-all(f32[8,4,64,128]{3,2,1,0:T(8,128)S(1)} %add_cores.1), channel_id=1, replica_groups=mesh['freq'=8,'y_high'=4,'y_low'=2,'x'=4,'core'=2] {'y_low','x'}, dimensions={0} | all-to-all | bytes 2097152 | tf_op jit(solution)/shard_map/all_to_all | solution.py:295
  35.3 0.1 sum_near.2
  35.4 9.8 %all_to_all.46.ref = f32[4,64,128]{2,1,0:T(8,128)S(1)} all-to-all(f32[4,64,128]{2,1,0:T(8,128)S(1)} %sum_near.2), channel_id=1, replica_groups=mesh['freq'=8,'y_high'=4,'y_low'=2,'x'=4,'core'=2] {'y_high'}, dimensions={0} | all-to-all | bytes 262144 | tf_op jit(solution)/shard_map/all_to_all | solution.py:295
  45.2 9.6 %all_to_all.47.ref = f32[4,64,128]{2,1,0:T(8,128)S(1)} all-to-all(f32[4,64,128]{2,1,0:T(8,128)S(1)} %sum_far.2), channel_id=1, replica_groups=mesh['freq'=8,'y_high'=4,'y_low'=2,'x'=4,'core'=2] {'y_high'}, dimensions={0} | all-to-all | bytes 262144 | tf_op jit(solution)/shard_map/all_to_all | solution.py:295
  54.8 0.1 repeat_near.2
  54.8 15.8 %all_to_all.48.g_ref = f32[8,4,64,128]{3,2,1,0:T(8,128)S(1)} all-to-all(f32[8,4,64,128]{3,2,1,0:T(8,128)S(1)} %repeat_near.2), channel_id=1, replica_groups=mesh['freq'=8,'y_high'=4,'y_low'=2,'x'=4,'core'=2] {'y_low','x'}, dimensions={0} | all-to-all | bytes 2097152 | tf_op jit(solution)/shard_map/all_to_all | solution.py:295
  70.6 0.0 collective-permute-done.1.other_ref
  70.6 4.3 %normal_product.1 = (f32[8,4,64,128]{3,2,1,0:T(8,128)S(1)}, f32[512,128]{1,0:T(8,128)S(1)}) custom-call(f32[8,4,64,128]{3,2,1,0:T(8,128)S(1)} %all_to_all.48.g_ref, f32[2,2048,256]{2,1,0:T(8,128)S(1)} %get-tuple-element.16.own_ref, f32[2,2048,256]{2,1,0:T(8,128)S(1)} %collective-permute-done.1.other_ref), custom_call_target="tpu_custom_call" | custom-call | tf_op jit(solution)/shard_map/normal_product/pallas_call | solution.py:145
  74.9 13.2 %all_to_all.49.ref = f32[8,4,64,128]{3,2,1,0:T(8,128)S(1)} all-to-all(f32[8,4,64,128]{3,2,1,0:T(8,128)S(1)} %get-tuple-element.17), channel_id=1, replica_groups=mesh['freq'=8,'y_high'=4,'y_low'=2,'x'=4,'core'=2] {'y_low','x'}, dimensions={0} | all-to-all | bytes 2097152 | tf_op jit(solution)/shard_map/all_to_all | solution.py:295
  88.1 0.1 sum_near.3
  88.2 9.6 %all_to_all.50.ref = f32[4,64,128]{2,1,0:T(8,128)S(1)} all-to-all(f32[4,64,128]{2,1,0:T(8,128)S(1)} %sum_near.3), channel_id=1, replica_groups=mesh['freq'=8,'y_high'=4,'y_low'=2,'x'=4,'core'=2] {'y_high'}, dimensions={0} | all-to-all | bytes 262144 | tf_op jit(solution)/shard_map/all_to_all | solution.py:295
  97.8 9.6 %all_to_all.51.ref = f32[4,64,128]{2,1,0:T(8,128)S(1)} all-to-all(f32[4,64,128]{2,1,0:T(8,128)S(1)} %sum_far.3), channel_id=1, replica_groups=mesh['freq'=8,'y_high'=4,'y_low'=2,'x'=4,'core'=2] {'y_high'}, dimensions={0} | all-to-all | bytes 262144 | tf_op jit(solution)/shard_map/all_to_all | solution.py:295
  107.5 0.1 repeat_near.3
  107.5 13.5 %all_to_all.52.q_ref = f32[8,4,64,128]{3,2,1,0:T(8,128)S(1)} all-to-all(f32[8,4,64,128]{3,2,1,0:T(8,128)S(1)} %repeat_near.3), channel_id=1, replica_groups=mesh['freq'=8,'y_high'=4,'y_low'=2,'x'=4,'core'=2] {'y_low','x'}, dimensions={0} | all-to-all | bytes 2097152 | tf_op jit(solution)/shard_map/all_to_all | solution.py:295
  121.0 0.0 copy-start
  121.0 3.0 %second_forward.1 = (f32[576,128]{1,0:T(8,128)S(1)}, f32[576,128]{1,0:T(8,128)S(1)}, f32[64,1,128]{2,1,0:T(1,128)S(1)}) custom-call(f32[8,4,64,128]{3,2,1,0:T(8,128)S(1)} %all_to_all.48.g_ref, f32[8,4,64,128]{3,2,1,0:T(8,128)S(1)} %all_to_all.52.q_ref, f32[2,2048,256]{2,1,0:T(8,128)S(1)} %get-tuple-element.16.own_ref, ...), custom_call_target="tpu_custom_call" | custom-call | tf_op jit(solution)/shard_map/second_forward/pallas_call | solution.py:192
  124.1 12.5 %collective-permute-start.2 = (f32[576,128]{1,0:T(8,128)S(1)}, f32[576,128]{1,0:T(8,128)S(1)}, u32[]{:S(2)}, u32[]{:S(2)}) collective-permute-start(f32[576,128]{1,0:T(8,128)S(1)} %get-tuple-element.21), channel_id=1, source_target_pairs={{0,1},{1,0},{2,3},{3,2},{4,5},{5,4},{6,7},{7,6},{8,9},{9,8},{10,11... | collective-permute-start | bytes 884744 | tf_op jit(solution)/shard_map/ppermute | solution.py:314
  136.6 12.7 %all_to_all.53.got_ref = f32[64,1,128]{2,1,0:T(1,128)S(1)} all-to-all(f32[64,1,128]{2,1,0:T(1,128)S(1)} %get-tuple-element.19), channel_id=1, replica_groups=mesh['freq'=8,'y_high'=4,'y_low'=2,'x'=4,'core'=2] {'y_high','y_low','x'..., dimensions={0} | all-to-all | bytes 65536 | tf_op jit(solution)/shard_map/all_to_all | solution.py:315
  149.3 0.0 collective-permute-done.2.take_ref
  149.3 0.0 copy-done
  149.3 1.2 last_update.1
  (2 shorter events, 0.0 us)
Async XLA Ops:
  4.7 11.1 %collective-permute-start = (f32[8,4,64,128]{3,2,1,0:T(8,128)S(1)}, f32[8,4,64,128]{3,2,1,0:T(8,128)S(1)}, u32[]{:S(2)}, u32[]{:S(2)}) collective-permute-start(f32[8,4,64,128]{3,2,1,0:T(8,128)S(1)} %get-tuple-element.14), channel_id=1, source_target_pairs={{0,1},{1,0},{2,3},{3,2},{4,5},{5,4},{6,7},{7,6},{8,9},{9,8},{10,11... | collective-permute-start | bytes 3145736 | tf_op jit(solution)/shard_map/ppermute | solution.py:307
  15.8 54.8 %collective-permute-start.1 = (f32[2,2048,256]{2,1,0:T(8,128)S(1)}, f32[2,2048,256]{2,1,0:T(8,128)S(1)}, u32[]{:S(2)}, u32[]{:S(2)}) collective-permute-start(f32[2,2048,256]{2,1,0:T(8,128)S(1)} %get-tuple-element.16.own_ref), channel_id=1, source_target_pairs={{0,1},{1,0},{2,3},{3,2},{4,5},{5,4},{6,7},{7,6},{8,9},{9,8},{10,11... | collective-permute-start | bytes 12582920 | tf_op jit(solution)/shard_map/ppermute | solution.py:309
  121.0 28.3 %copy-start = (f32[2,256,128]{2,1,0:T(8,128)S(1)}, f32[2,256,128]{2,1,0:T(8,128)}, u32[]{:S(2)}) copy-start(f32[2,256,128]{2,1,0:T(8,128)} %up_ref.1) | copy-start | bytes 786436
  124.1 25.2 %collective-permute-start.2 = (f32[576,128]{1,0:T(8,128)S(1)}, f32[576,128]{1,0:T(8,128)S(1)}, u32[]{:S(2)}, u32[]{:S(2)}) collective-permute-start(f32[576,128]{1,0:T(8,128)S(1)} %get-tuple-element.21), channel_id=1, source_target_pairs={{0,1},{1,0},{2,3},{3,2},{4,5},{5,4},{6,7},{7,6},{8,9},{9,8},{10,11... | collective-permute-start | bytes 884744 | tf_op jit(solution)/shard_map/ppermute | solution.py:314

commit v6 on v5

--- a/solution.py
+++ b/solution.py
@@ -295,11 +295,19 @@
     return lax.all_to_all(blocks, axis, 0, 0, tiled=True)
 
 
-def all_sum(partial):
-    row = small(sum_kernel, partial.shape[1:], "sum_near", exchange(partial, NEAR))
-    row = small(sum_repeat_kernel, row.shape, "sum_far", exchange(row, "y_high"))
-    whole = small(repeat_kernel, partial.shape, "repeat_near", exchange(row, "y_high"))
-    return exchange(whole, NEAR)
+def far_one_step(row):
+    rows = small(repeat_kernel, (4,) + row.shape, "repeat_far", row)
+    return small(sum_kernel, row.shape, "sum_far", exchange(rows, "y_high"))
+
+
+def far_two_steps(row):
+    block = small(sum_repeat_kernel, row.shape, "sum_far", exchange(row, "y_high"))
+    return exchange(block, "y_high")
+
+
+def all_sum(partial, far):
+    row = far(small(sum_kernel, partial.shape[1:], "sum_near", exchange(partial, NEAR)))
+    return exchange(small(repeat_kernel, partial.shape, "repeat_near", row), NEAR)
 
 
 def on_device(downgoing, upgoing):
@@ -307,9 +315,9 @@
     theirs = lax.ppermute(theirs, SRC, SWAP)
     down, theirs = lax.optimization_barrier((down, theirs))
     other_down = lax.ppermute(down, SRC, SWAP)
-    g = all_sum(small(add_kernel, mine.shape, "add_cores", mine, theirs))
+    g = all_sum(small(add_kernel, mine.shape, "add_cores", mine, theirs), far_two_steps)
     q, image0 = normal(g, down, other_down)
-    q = all_sum(q)
+    q = all_sum(q, far_one_step)
     keep, give, row = second_forward(g, q, down, other_down, image0)
     take = lax.ppermute(give, SRC, SWAP)
     got = lax.all_to_all(row, SRC, 0, 0, tiled=True)

time: 151 us -> 143 us (0.947)
  blocking collectives: 111 us -> 106 us
  starting transfers between devices: 23.5 us -> 21.2 us
    all_to_all x8 -> x7, blocking collectives: 98.2 us -> 92.4 us  [exchange(): return lax.all_to_all(blocks, axis, 0, 0, tiled=True)]
    ppermute x1, starting transfers between devices: 12.5 us -> 10.1 us  [on_device(): take = lax.ppermute(give, SRC, SWAP)]
where the time goes in v6:
time: 143 us
  blocking collectives  106 us (74%)
  starting transfers between devices  21.2 us (15%)
  Pallas kernels  13.1 us (9%)
  waiting for transfers between devices  2.27 us (2%)
    all_to_all x7, blocking collectives, exchange(): return lax.all_to_all(blocks, axis, 0, 0, tiled=True)  92.4 us
    all_to_all x1, blocking collectives, on_device(): got = lax.all_to_all(row, SRC, 0, 0, tiled=True)  13.4 us
    ppermute x1, starting transfers between devices, on_device(): take = lax.ppermute(give, SRC, SWAP)  10.1 us
    ppermute x1, starting transfers between devices, on_device(): theirs = lax.ppermute(theirs, SRC, SWAP)  8.79 us
    pallas_call x1, Pallas kernels, normal(): pl.pallas_call(normal_kernel, in_specs=[VMEM, VMEM, VMEM], out_specs=(VME...  4.32 us
    pallas_call x1, Pallas kernels, first_adjoint(): pl.pallas_call(first_kernel, in_specs=[HBM, HBM], out_specs=(VMEM, VMEM,...  4.11 us
    pallas_call x1, Pallas kernels, second_forward(): pl.pallas_call(second_kernel, in_specs=[VMEM] * 5, out_specs=(VMEM,) * 3,...  3.03 us
  transfers between devices with their start and end apart: 3, of which 1 were waited for; matrix products, arithmetic and copies ran while one was open for 0% of the time, Pallas kernels for 0%

profile of v6, /device:TPU:1, one launch (start us, length us, event | category | flops | bytes accessed | tf_op | source)
XLA Modules:
  0.0 143.0 jit_solution(16449283096170848982)
XLA Ops:
  0.6 4.1 %first_adjoint.1 = (f32[8,4,64,128]{3,2,1,0:T(8,128)S(1)}, f32[8,4,64,128]{3,2,1,0:T(8,128)S(1)}, f32[2,2048,256]{2,1,0:T(8,128)S(1)}) custom-call(f32[2,2048,256]{2,1,0:T(8,128)} %down_hbm.1, f32[2,256,128]{2,1,0:T(8,128)} %up_ref.1), custom_call_target="tpu_custom_call" | custom-call | tf_op jit(solution)/shard_map/first_adjoint/pallas_call | solution.py:91
  4.7 8.8 %collective-permute-start = (f32[8,4,64,128]{3,2,1,0:T(8,128)S(1)}, f32[8,4,64,128]{3,2,1,0:T(8,128)S(1)}, u32[]{:S(2)}, u32[]{:S(2)}) collective-permute-start(f32[8,4,64,128]{3,2,1,0:T(8,128)S(1)} %get-tuple-element.14), channel_id=1, source_target_pairs={{0,1},{1,0},{2,3},{3,2},{4,5},{5,4},{6,7},{7,6},{8,9},{9,8},{10,11... | collective-permute-start | bytes 3145736 | tf_op jit(solution)/shard_map/ppermute | solution.py:315
  13.5 2.3 %collective-permute-done.b_ref = f32[8,4,64,128]{3,2,1,0:T(8,128)S(1)} collective-permute-done((f32[8,4,64,128]{3,2,1,0:T(8,128)S(1)}, f32[8,4,64,128]{3,2,1,0:T(8,128)S(1)}, u32[]{:S(2)}, u32[]{:S(2)}) %collective-permute-start) | collective-permute-done | bytes 1048608 | tf_op jit(solution)/shard_map/ppermute | solution.py:315
  15.8 2.3 %collective-permute-start.1 = (f32[2,2048,256]{2,1,0:T(8,128)S(1)}, f32[2,2048,256]{2,1,0:T(8,128)S(1)}, u32[]{:S(2)}, u32[]{:S(2)}) collective-permute-start(f32[2,2048,256]{2,1,0:T(8,128)S(1)} %get-tuple-element.16.own_ref), channel_id=1, source_target_pairs={{0,1},{1,0},{2,3},{3,2},{4,5},{5,4},{6,7},{7,6},{8,9},{9,8},{10,11... | collective-permute-start | bytes 12582920 | tf_op jit(solution)/shard_map/ppermute | solution.py:317
  18.1 0.1 add_cores.1
  18.2 17.1 %all_to_all.40.ref = f32[8,4,64,128]{3,2,1,0:T(8,128)S(1)} all-to-all(f32[8,4,64,128]{3,2,1,0:T(8,128)S(1)} %add_cores.1), channel_id=1, replica_groups=mesh['freq'=8,'y_high'=4,'y_low'=2,'x'=4,'core'=2] {'y_low','x'}, dimensions={0} | all-to-all | bytes 2097152 | tf_op jit(solution)/shard_map/all_to_all | solution.py:295
  35.3 0.1 sum_near.2
  35.4 9.8 %all_to_all.41.ref = f32[4,64,128]{2,1,0:T(8,128)S(1)} all-to-all(f32[4,64,128]{2,1,0:T(8,128)S(1)} %sum_near.2), channel_id=1, replica_groups=mesh['freq'=8,'y_high'=4,'y_low'=2,'x'=4,'core'=2] {'y_high'}, dimensions={0} | all-to-all | bytes 262144 | tf_op jit(solution)/shard_map/all_to_all | solution.py:295
  45.2 9.6 %all_to_all.42.ref = f32[4,64,128]{2,1,0:T(8,128)S(1)} all-to-all(f32[4,64,128]{2,1,0:T(8,128)S(1)} %sum_far.2), channel_id=1, replica_groups=mesh['freq'=8,'y_high'=4,'y_low'=2,'x'=4,'core'=2] {'y_high'}, dimensions={0} | all-to-all | bytes 262144 | tf_op jit(solution)/shard_map/all_to_all | solution.py:295
  54.8 0.1 repeat_near.2
  54.8 15.8 %all_to_all.43.g_ref = f32[8,4,64,128]{3,2,1,0:T(8,128)S(1)} all-to-all(f32[8,4,64,128]{3,2,1,0:T(8,128)S(1)} %repeat_near.2), channel_id=1, replica_groups=mesh['freq'=8,'y_high'=4,'y_low'=2,'x'=4,'core'=2] {'y_low','x'}, dimensions={0} | all-to-all | bytes 2097152 | tf_op jit(solution)/shard_map/all_to_all | solution.py:295
  70.6 0.0 collective-permute-done.1.other_ref
  70.6 4.3 %normal_product.1 = (f32[8,4,64,128]{3,2,1,0:T(8,128)S(1)}, f32[512,128]{1,0:T(8,128)S(1)}) custom-call(f32[8,4,64,128]{3,2,1,0:T(8,128)S(1)} %all_to_all.43.g_ref, f32[2,2048,256]{2,1,0:T(8,128)S(1)} %get-tuple-element.16.own_ref, f32[2,2048,256]{2,1,0:T(8,128)S(1)} %collective-permute-done.1.other_ref), custom_call_target="tpu_custom_call" | custom-call | tf_op jit(solution)/shard_map/normal_product/pallas_call | solution.py:145
  74.9 13.2 %all_to_all.44.ref = f32[8,4,64,128]{3,2,1,0:T(8,128)S(1)} all-to-all(f32[8,4,64,128]{3,2,1,0:T(8,128)S(1)} %get-tuple-element.17), channel_id=1, replica_groups=mesh['freq'=8,'y_high'=4,'y_low'=2,'x'=4,'core'=2] {'y_low','x'}, dimensions={0} | all-to-all | bytes 2097152 | tf_op jit(solution)/shard_map/all_to_all | solution.py:295
  88.1 0.1 sum_near.3.ref
  88.2 13.2 %all_to_all.45.ref = f32[4,4,64,128]{3,2,1,0:T(8,128)S(1)} all-to-all(f32[4,4,64,128]{3,2,1,0:T(8,128)S(1)} %repeat_far.1), channel_id=1, replica_groups=mesh['freq'=8,'y_high'=4,'y_low'=2,'x'=4,'core'=2] {'y_high'}, dimensions={0} | all-to-all | bytes 1048576 | tf_op jit(solution)/shard_map/all_to_all | solution.py:295
  101.4 0.1 repeat_near.3
  101.5 13.7 %all_to_all.46.q_ref = f32[8,4,64,128]{3,2,1,0:T(8,128)S(1)} all-to-all(f32[8,4,64,128]{3,2,1,0:T(8,128)S(1)} %repeat_near.3), channel_id=1, replica_groups=mesh['freq'=8,'y_high'=4,'y_low'=2,'x'=4,'core'=2] {'y_low','x'}, dimensions={0} | all-to-all | bytes 2097152 | tf_op jit(solution)/shard_map/all_to_all | solution.py:295
  115.2 0.0 copy-start
  115.2 3.0 %second_forward.1 = (f32[576,128]{1,0:T(8,128)S(1)}, f32[576,128]{1,0:T(8,128)S(1)}, f32[64,1,128]{2,1,0:T(1,128)S(1)}) custom-call(f32[8,4,64,128]{3,2,1,0:T(8,128)S(1)} %all_to_all.43.g_ref, f32[8,4,64,128]{3,2,1,0:T(8,128)S(1)} %all_to_all.46.q_ref, f32[2,2048,256]{2,1,0:T(8,128)S(1)} %get-tuple-element.16.own_ref, ...), custom_call_target="tpu_custom_call" | custom-call | tf_op jit(solution)/shard_map/second_forward/pallas_call | solution.py:192
  118.3 10.1 %collective-permute-start.2 = (f32[576,128]{1,0:T(8,128)S(1)}, f32[576,128]{1,0:T(8,128)S(1)}, u32[]{:S(2)}, u32[]{:S(2)}) collective-permute-start(f32[576,128]{1,0:T(8,128)S(1)} %get-tuple-element.21), channel_id=1, source_target_pairs={{0,1},{1,0},{2,3},{3,2},{4,5},{5,4},{6,7},{7,6},{8,9},{9,8},{10,11... | collective-permute-start | bytes 884744 | tf_op jit(solution)/shard_map/ppermute | solution.py:322
  128.4 13.4 %all_to_all.47.got_ref = f32[64,1,128]{2,1,0:T(1,128)S(1)} all-to-all(f32[64,1,128]{2,1,0:T(1,128)S(1)} %get-tuple-element.19), channel_id=1, replica_groups=mesh['freq'=8,'y_high'=4,'y_low'=2,'x'=4,'core'=2] {'y_high','y_low','x'..., dimensions={0} | all-to-all | bytes 65536 | tf_op jit(solution)/shard_map/all_to_all | solution.py:323
  141.8 0.0 collective-permute-done.2.take_ref
  141.8 0.0 copy-done
  141.8 1.2 last_update.1
  (3 shorter events, 0.1 us)
Async XLA Ops:
  4.7 11.1 %collective-permute-start = (f32[8,4,64,128]{3,2,1,0:T(8,128)S(1)}, f32[8,4,64,128]{3,2,1,0:T(8,128)S(1)}, u32[]{:S(2)}, u32[]{:S(2)}) collective-permute-start(f32[8,4,64,128]{3,2,1,0:T(8,128)S(1)} %get-tuple-element.14), channel_id=1, source_target_pairs={{0,1},{1,0},{2,3},{3,2},{4,5},{5,4},{6,7},{7,6},{8,9},{9,8},{10,11... | collective-permute-start | bytes 3145736 | tf_op jit(solution)/shard_map/ppermute | solution.py:315
  15.8 54.8 %collective-permute-start.1 = (f32[2,2048,256]{2,1,0:T(8,128)S(1)}, f32[2,2048,256]{2,1,0:T(8,128)S(1)}, u32[]{:S(2)}, u32[]{:S(2)}) collective-permute-start(f32[2,2048,256]{2,1,0:T(8,128)S(1)} %get-tuple-element.16.own_ref), channel_id=1, source_target_pairs={{0,1},{1,0},{2,3},{3,2},{4,5},{5,4},{6,7},{7,6},{8,9},{9,8},{10,11... | collective-permute-start | bytes 12582920 | tf_op jit(solution)/shard_map/ppermute | solution.py:317
  115.2 26.5 %copy-start = (f32[2,256,128]{2,1,0:T(8,128)S(1)}, f32[2,256,128]{2,1,0:T(8,128)}, u32[]{:S(2)}) copy-start(f32[2,256,128]{2,1,0:T(8,128)} %up_ref.1) | copy-start | bytes 786436
  118.3 23.5 %collective-permute-start.2 = (f32[576,128]{1,0:T(8,128)S(1)}, f32[576,128]{1,0:T(8,128)S(1)}, u32[]{:S(2)}, u32[]{:S(2)}) collective-permute-start(f32[576,128]{1,0:T(8,128)S(1)} %get-tuple-element.21), channel_id=1, source_target_pairs={{0,1},{1,0},{2,3},{3,2},{4,5},{5,4},{6,7},{7,6},{8,9},{9,8},{10,11... | collective-permute-start | bytes 884744 | tf_op jit(solution)/shard_map/ppermute | solution.py:322

commit v7 on v6

--- a/solution.py
+++ b/solution.py
@@ -312,10 +312,10 @@
 
 def on_device(downgoing, upgoing):
     mine, theirs, down = first_adjoint(downgoing, upgoing)
+    other_down = lax.ppermute(down, SRC, SWAP)
     theirs = lax.ppermute(theirs, SRC, SWAP)
-    down, theirs = lax.optimization_barrier((down, theirs))
-    other_down = lax.ppermute(down, SRC, SWAP)
     g = all_sum(small(add_kernel, mine.shape, "add_cores", mine, theirs), far_two_steps)
+    g, down = lax.optimization_barrier((g, down))
     q, image0 = normal(g, down, other_down)
     q = all_sum(q, far_one_step)
     keep, give, row = second_forward(g, q, down, other_down, image0)

time: 143 us -> 140 us (0.979)
  blocking collectives: 106 us -> 104 us
  waiting for transfers between devices: 2.27 us -> 0.34 us
    ppermute x1, waiting for transfers between devices: 2.26 us -> 0.34 us  [on_device(): theirs = lax.ppermute(theirs, SRC, SWAP)]
where the time goes in v7:
time: 140 us
  blocking collectives  104 us (74%)
  starting transfers between devices  21.9 us (16%)
  Pallas kernels  13.1 us (9%)
    all_to_all x7, blocking collectives, exchange(): return lax.all_to_all(blocks, axis, 0, 0, tiled=True)  91.2 us
    all_to_all x1, blocking collectives, on_device(): got = lax.all_to_all(row, SRC, 0, 0, tiled=True)  12.7 us
    ppermute x1, starting transfers between devices, on_device(): take = lax.ppermute(give, SRC, SWAP)  11.2 us
    ppermute x1, starting transfers between devices, on_device(): theirs = lax.ppermute(theirs, SRC, SWAP)  8.79 us
    pallas_call x1, Pallas kernels, normal(): pl.pallas_call(normal_kernel, in_specs=[VMEM, VMEM, VMEM], out_specs=(VME...  4.32 us
    pallas_call x1, Pallas kernels, first_adjoint(): pl.pallas_call(first_kernel, in_specs=[HBM, HBM], out_specs=(VMEM, VMEM,...  4.11 us
    pallas_call x1, Pallas kernels, second_forward(): pl.pallas_call(second_kernel, in_specs=[VMEM] * 5, out_specs=(VMEM,) * 3,...  3.04 us
  transfers between devices with their start and end apart: 3, of which 1 were waited for; matrix products, arithmetic and copies ran while one was open for 0% of the time, Pallas kernels for 0%

profile of v7, /device:TPU:1, one launch (start us, length us, event | category | flops | bytes accessed | tf_op | source)
XLA Modules:
  0.0 140.0 jit_solution(9904560259662838649)
XLA Ops:
  0.6 4.1 %first_adjoint.1 = (f32[8,4,64,128]{3,2,1,0:T(8,128)S(1)}, f32[8,4,64,128]{3,2,1,0:T(8,128)S(1)}, f32[2,2048,256]{2,1,0:T(8,128)S(1)}) custom-call(f32[2,2048,256]{2,1,0:T(8,128)} %down_hbm.1, f32[2,256,128]{2,1,0:T(8,128)} %up_ref.1), custom_call_target="tpu_custom_call" | custom-call | tf_op jit(solution)/shard_map/first_adjoint/pallas_call | solution.py:91
  4.7 8.8 %collective-permute-start = (f32[8,4,64,128]{3,2,1,0:T(8,128)S(1)}, f32[8,4,64,128]{3,2,1,0:T(8,128)S(1)}, u32[]{:S(2)}, u32[]{:S(2)}) collective-permute-start(f32[8,4,64,128]{3,2,1,0:T(8,128)S(1)} %get-tuple-element.13), channel_id=1, source_target_pairs={{0,1},{1,0},{2,3},{3,2},{4,5},{5,4},{6,7},{7,6},{8,9},{9,8},{10,11... | collective-permute-start | bytes 3145736 | tf_op jit(solution)/shard_map/ppermute | solution.py:316
  13.5 1.9 %collective-permute-start.1 = (f32[2,2048,256]{2,1,0:T(8,128)S(1)}, f32[2,2048,256]{2,1,0:T(8,128)S(1)}, u32[]{:S(2)}, u32[]{:S(2)}) collective-permute-start(f32[2,2048,256]{2,1,0:T(8,128)S(1)} %get-tuple-element.16.own_ref), channel_id=1, source_target_pairs={{0,1},{1,0},{2,3},{3,2},{4,5},{5,4},{6,7},{7,6},{8,9},{9,8},{10,11... | collective-permute-start | bytes 12582920 | tf_op jit(solution)/shard_map/ppermute | solution.py:315
  15.5 0.3 collective-permute-done.b_ref
  15.8 0.1 add_cores.1
  15.9 16.9 %all_to_all.40.ref = f32[8,4,64,128]{3,2,1,0:T(8,128)S(1)} all-to-all(f32[8,4,64,128]{3,2,1,0:T(8,128)S(1)} %add_cores.1), channel_id=1, replica_groups=mesh['freq'=8,'y_high'=4,'y_low'=2,'x'=4,'core'=2] {'y_low','x'}, dimensions={0} | all-to-all | bytes 2097152 | tf_op jit(solution)/shard_map/all_to_all | solution.py:295
  32.8 0.1 sum_near.2
  32.9 10.1 %all_to_all.41.ref = f32[4,64,128]{2,1,0:T(8,128)S(1)} all-to-all(f32[4,64,128]{2,1,0:T(8,128)S(1)} %sum_near.2), channel_id=1, replica_groups=mesh['freq'=8,'y_high'=4,'y_low'=2,'x'=4,'core'=2] {'y_high'}, dimensions={0} | all-to-all | bytes 262144 | tf_op jit(solution)/shard_map/all_to_all | solution.py:295
  42.9 9.6 %all_to_all.42.ref = f32[4,64,128]{2,1,0:T(8,128)S(1)} all-to-all(f32[4,64,128]{2,1,0:T(8,128)S(1)} %sum_far.2), channel_id=1, replica_groups=mesh['freq'=8,'y_high'=4,'y_low'=2,'x'=4,'core'=2] {'y_high'}, dimensions={0} | all-to-all | bytes 262144 | tf_op jit(solution)/shard_map/all_to_all | solution.py:295
  52.5 0.1 repeat_near.2
  52.6 13.9 %all_to_all.43.g_ref = f32[8,4,64,128]{3,2,1,0:T(8,128)S(1)} all-to-all(f32[8,4,64,128]{3,2,1,0:T(8,128)S(1)} %repeat_near.2), channel_id=1, replica_groups=mesh['freq'=8,'y_high'=4,'y_low'=2,'x'=4,'core'=2] {'y_low','x'}, dimensions={0} | all-to-all | bytes 2097152 | tf_op jit(solution)/shard_map/all_to_all | solution.py:295
  66.5 0.0 collective-permute-done.1.other_ref
  66.5 4.3 %normal_product.1 = (f32[8,4,64,128]{3,2,1,0:T(8,128)S(1)}, f32[512,128]{1,0:T(8,128)S(1)}) custom-call(f32[8,4,64,128]{3,2,1,0:T(8,128)S(1)} %all_to_all.43.g_ref, f32[2,2048,256]{2,1,0:T(8,128)S(1)} %get-tuple-element.16.own_ref, f32[2,2048,256]{2,1,0:T(8,128)S(1)} %collective-permute-done.1.other_ref), custom_call_target="tpu_custom_call" | custom-call | tf_op jit(solution)/shard_map/normal_product/pallas_call | solution.py:145
  70.8 13.9 %all_to_all.44.ref = f32[8,4,64,128]{3,2,1,0:T(8,128)S(1)} all-to-all(f32[8,4,64,128]{3,2,1,0:T(8,128)S(1)} %get-tuple-element.17), channel_id=1, replica_groups=mesh['freq'=8,'y_high'=4,'y_low'=2,'x'=4,'core'=2] {'y_low','x'}, dimensions={0} | all-to-all | bytes 2097152 | tf_op jit(solution)/shard_map/all_to_all | solution.py:295
  84.7 0.1 sum_near.3.ref
  84.8 13.3 %all_to_all.45.ref = f32[4,4,64,128]{3,2,1,0:T(8,128)S(1)} all-to-all(f32[4,4,64,128]{3,2,1,0:T(8,128)S(1)} %repeat_far.1), channel_id=1, replica_groups=mesh['freq'=8,'y_high'=4,'y_low'=2,'x'=4,'core'=2] {'y_high'}, dimensions={0} | all-to-all | bytes 1048576 | tf_op jit(solution)/shard_map/all_to_all | solution.py:295
  98.1 0.1 repeat_near.3
  98.2 13.6 %all_to_all.46.q_ref = f32[8,4,64,128]{3,2,1,0:T(8,128)S(1)} all-to-all(f32[8,4,64,128]{3,2,1,0:T(8,128)S(1)} %repeat_near.3), channel_id=1, replica_groups=mesh['freq'=8,'y_high'=4,'y_low'=2,'x'=4,'core'=2] {'y_low','x'}, dimensions={0} | all-to-all | bytes 2097152 | tf_op jit(solution)/shard_map/all_to_all | solution.py:295
  111.8 0.0 copy-start
  111.8 3.0 %second_forward.1 = (f32[576,128]{1,0:T(8,128)S(1)}, f32[576,128]{1,0:T(8,128)S(1)}, f32[64,1,128]{2,1,0:T(1,128)S(1)}) custom-call(f32[8,4,64,128]{3,2,1,0:T(8,128)S(1)} %all_to_all.43.g_ref, f32[8,4,64,128]{3,2,1,0:T(8,128)S(1)} %all_to_all.46.q_ref, f32[2,2048,256]{2,1,0:T(8,128)S(1)} %get-tuple-element.16.own_ref, ...), custom_call_target="tpu_custom_call" | custom-call | tf_op jit(solution)/shard_map/second_forward/pallas_call | solution.py:192
  114.8 11.2 %collective-permute-start.2 = (f32[576,128]{1,0:T(8,128)S(1)}, f32[576,128]{1,0:T(8,128)S(1)}, u32[]{:S(2)}, u32[]{:S(2)}) collective-permute-start(f32[576,128]{1,0:T(8,128)S(1)} %get-tuple-element.21), channel_id=1, source_target_pairs={{0,1},{1,0},{2,3},{3,2},{4,5},{5,4},{6,7},{7,6},{8,9},{9,8},{10,11... | collective-permute-start | bytes 884744 | tf_op jit(solution)/shard_map/ppermute | solution.py:322
  126.0 12.7 %all_to_all.47.got_ref = f32[64,1,128]{2,1,0:T(1,128)S(1)} all-to-all(f32[64,1,128]{2,1,0:T(1,128)S(1)} %get-tuple-element.19), channel_id=1, replica_groups=mesh['freq'=8,'y_high'=4,'y_low'=2,'x'=4,'core'=2] {'y_high','y_low','x'..., dimensions={0} | all-to-all | bytes 65536 | tf_op jit(solution)/shard_map/all_to_all | solution.py:323
  138.8 0.0 collective-permute-done.2.take_ref
  138.8 0.0 copy-done
  138.8 1.2 last_update.1
  (3 shorter events, 0.1 us)
Async XLA Ops:
  4.7 11.1 %collective-permute-start = (f32[8,4,64,128]{3,2,1,0:T(8,128)S(1)}, f32[8,4,64,128]{3,2,1,0:T(8,128)S(1)}, u32[]{:S(2)}, u32[]{:S(2)}) collective-permute-start(f32[8,4,64,128]{3,2,1,0:T(8,128)S(1)} %get-tuple-element.13), channel_id=1, source_target_pairs={{0,1},{1,0},{2,3},{3,2},{4,5},{5,4},{6,7},{7,6},{8,9},{9,8},{10,11... | collective-permute-start | bytes 3145736 | tf_op jit(solution)/shard_map/ppermute | solution.py:316
  13.5 53.0 %collective-permute-start.1 = (f32[2,2048,256]{2,1,0:T(8,128)S(1)}, f32[2,2048,256]{2,1,0:T(8,128)S(1)}, u32[]{:S(2)}, u32[]{:S(2)}) collective-permute-start(f32[2,2048,256]{2,1,0:T(8,128)S(1)} %get-tuple-element.16.own_ref), channel_id=1, source_target_pairs={{0,1},{1,0},{2,3},{3,2},{4,5},{5,4},{6,7},{7,6},{8,9},{9,8},{10,11... | collective-permute-start | bytes 12582920 | tf_op jit(solution)/shard_map/ppermute | solution.py:315
  111.8 27.0 %copy-start = (f32[2,256,128]{2,1,0:T(8,128)S(1)}, f32[2,256,128]{2,1,0:T(8,128)}, u32[]{:S(2)}) copy-start(f32[2,256,128]{2,1,0:T(8,128)} %up_ref.1) | copy-start | bytes 786436
  114.8 23.9 %collective-permute-start.2 = (f32[576,128]{1,0:T(8,128)S(1)}, f32[576,128]{1,0:T(8,128)S(1)}, u32[]{:S(2)}, u32[]{:S(2)}) collective-permute-start(f32[576,128]{1,0:T(8,128)S(1)} %get-tuple-element.21), channel_id=1, source_target_pairs={{0,1},{1,0},{2,3},{3,2},{4,5},{5,4},{6,7},{7,6},{8,9},{9,8},{10,11... | collective-permute-start | bytes 884744 | tf_op jit(solution)/shard_map/ppermute | solution.py:322
